TPU v7x, 128 devices: a whole 4x4x4 slice. The times are simulated.
128 devices in a mesh: blk: 4 (over x), tok: 32 (over y, z, core).
Axes of the slice: x: 4, y: 4, z: 4, core: 2. Of those that a mesh axis runs over, the one named last changes fastest.
Arguments:
- inputs: bfloat16 [16384, 2048], P(('blk', 'tok')), may hold values from -6 to 6
- mix_scale: bfloat16 [2048], P('tok'), may hold values from 0.5 to 1.5
- branch_mat: bfloat16 [2048, 2560], P('tok', 'blk'), may hold values from -0.125 to 0.125
- input_mat: bfloat16 [2048, 2560], P('tok', 'blk'), may hold values from -0.125 to 0.125
- conv_taps: bfloat16 [4, 2560], P(None, ('blk', 'tok')), may hold values from -3 to 3
- conv_shift: bfloat16 [2560], P(('blk', 'tok')), may hold values from -2 to 2
- rate_mat: bfloat16 [16, 160, 160], P('blk', 'tok'), may hold values from -0.5 to 0.5
- rate_shift: bfloat16 [2560], P(('blk', 'tok')), may hold values from -2 to 2
- entry_mat: bfloat16 [16, 160, 160], P('blk', 'tok'), may hold values from -0.5 to 0.5
- entry_shift: bfloat16 [2560], P(('blk', 'tok')), may hold values from -2 to 2
- decay_logit: bfloat16 [2560], P(('blk', 'tok')), may hold values from 5 to 14
- out_mat: bfloat16 [2560, 2048], P('blk', 'tok'), may hold values from -0.25 to 0.25
- feed_scale: bfloat16 [2048], P('tok'), may hold values from 0.5 to 1.5
- gate_mat: bfloat16 [2048, 6144], P('tok', 'blk'), may hold values from -0.125 to 0.125
- up_mat: bfloat16 [2048, 6144], P('tok', 'blk'), may hold values from -0.125 to 0.125
- down_mat: bfloat16 [6144, 2048], P('blk', 'tok'), may hold values from -0.15625 to 0.15625
- lengths: int32 [5], replicated, may hold values from 1024 to 8192, as said below
- cotangent: bfloat16 [16384, 2048], P(('blk', 'tok')), may hold values from -6 to 6
Outputs:
- layer_out: bfloat16 [16384, 2048], P(('blk', 'tok'))
- inputs_grad: bfloat16 [16384, 2048], P(('blk', 'tok'))
- mix_scale_grad: float32 [2048], P('tok')
- branch_mat_grad: float32 [2048, 2560], P('tok', 'blk')
- input_mat_grad: float32 [2048, 2560], P('tok', 'blk')
- conv_taps_grad: float32 [4, 2560], P(None, ('blk', 'tok'))
- conv_shift_grad: float32 [2560], P(('blk', 'tok'))
- rate_mat_grad: float32 [16, 160, 160], P('blk', 'tok')
- rate_shift_grad: float32 [2560], P(('blk', 'tok'))
- entry_mat_grad: float32 [16, 160, 160], P('blk', 'tok')
- entry_shift_grad: float32 [2560], P(('blk', 'tok'))
- decay_logit_grad: float32 [2560], P(('blk', 'tok'))
- out_mat_grad: float32 [2560, 2048], P('blk', 'tok')
- feed_scale_grad: float32 [2048], P('tok')
- gate_mat_grad: float32 [2048, 6144], P('tok', 'blk')
- up_mat_grad: float32 [2048, 6144], P('tok', 'blk')
- down_mat_grad: float32 [6144, 2048], P('blk', 'tok')
Inputs may be any that keep to these rules, and one draw needn't show every extreme that they name: `lengths`: token counts of the items laid end to end in this order; they sum to 16384, and one item has exactly 8192 tokens.
All inputs are finite; a program needn't handle non-finite values.
Results may differ from a plain program's by a relative error of at most 0.023.
Values may be sent and summed in bfloat16 or wider, within the bound.
No kernel may reach another device: no remote copies, remote signals or barrier semaphores. Data moves between devices by JAX's collectives and lax.ppermute only.
A program may use at most 192 MiB of HBM per device.

v0:
```python
import jax
import jax.numpy as jnp
from jax import lax
from jax.sharding import PartitionSpec as P

CONV = 4


eps_norm = 1e-06
decay_power = 8.0
highest = lax.Precision.HIGHEST


def shifted_2(block, axis, distance):
    devices = range(lax.axis_size(axis))
    route = [((i - distance) % len(devices), i) for i in devices]
    return lax.ppermute(block, axis, route)


def compose(former, latter):
    return (former[0] * latter[0], former[1] * latter[0] + latter[1])


def product(operand, weight):
    return jnp.dot(operand, weight, preferred_element_type=jnp.float32)


def product_back(operand, weight):
    return lax.dot_general(
        operand, weight, (((1,), (1,)), ((), ())), preferred_element_type=jnp.float32
    )


def product_outer(operand, weight):
    return lax.dot_general(
        operand, weight, (((0,), (0,)), ((), ())), preferred_element_type=jnp.float32
    )


def normalize(values, gains):
    factor = lax.rsqrt(jnp.mean(values * values, axis=1, keepdims=True) + eps_norm)
    return (values * factor * gains, factor)


def normalize_back(gradient, values, factor, gains):
    weighted = gradient * gains
    partial_value = jnp.sum(gradient * values * factor, axis=0)
    backward = factor * weighted - values * (factor * factor * factor) * jnp.mean(
        weighted * values, axis=1, keepdims=True
    )
    return (backward, partial_value)


def spread_rows(values):
    return lax.all_gather(values, "blk", axis=0, tiled=True)


def spread_grads(values):
    return lax.all_gather(values, "blk", axis=0, tiled=True)


def settle(products):
    pieces = []
    for operand, weight, turned in products:
        pieces.append(product_back(operand, weight) if turned else product(operand, weight))
    running = pieces[0]
    for further in pieces[1:]:
        running = running + further
    return lax.psum_scatter(running, "blk", scatter_dimension=0, tiled=True)


def boundary_carry(coeffs, values, backward):
    gathered = (
        lax.all_gather(coeffs[None], "tok", axis=0, tiled=True),
        lax.all_gather(values[None], "tok", axis=0, tiled=True),
    )
    tok_width = gathered[0].shape[0]
    ordered = tuple(
        (jnp.swapaxes(member, 0, 1).reshape(-1, member.shape[-1]) for member in gathered)
    )
    if backward:
        ordered = tuple((jnp.flip(member, 0) for member in ordered))
    folded = lax.associative_scan(compose, ordered, axis=0)
    shifted = jnp.concatenate([jnp.zeros_like(folded[1][:1]), folded[1][:-1]], axis=0)
    if backward:
        shifted = jnp.flip(shifted, 0)
    picked = jnp.arange(coeffs.shape[0], dtype=jnp.int32) * tok_width + lax.axis_index("tok")
    return jnp.take(shifted, picked, axis=0)


def per_device(
    inputs,
    mix_scale,
    branch_mat,
    input_mat,
    conv_taps,
    conv_shift,
    rate_mat,
    rate_shift,
    entry_mat,
    entry_shift,
    decay_logit,
    out_mat,
    feed_scale,
    gate_mat,
    up_mat,
    down_mat,
    lengths,
    cotangent,
):
    own_rows = inputs.shape[0]
    tok_total = lax.axis_size("tok")
    tok_place = lax.axis_index("tok")
    members = lax.axis_size("blk")
    fetched = (
        lax.all_gather(mix_scale, "tok", axis=0, tiled=True),
        lax.all_gather(branch_mat, "tok", axis=0, tiled=True),
        lax.all_gather(input_mat, "tok", axis=0, tiled=True),
        lax.all_gather(conv_taps, "tok", axis=1, tiled=True),
        lax.all_gather(conv_shift, "tok", axis=0, tiled=True),
        lax.all_gather(rate_mat, "tok", axis=1, tiled=True),
        lax.all_gather(rate_shift, "tok", axis=0, tiled=True),
        lax.all_gather(entry_mat, "tok", axis=1, tiled=True),
        lax.all_gather(entry_shift, "tok", axis=0, tiled=True),
        lax.all_gather(decay_logit, "tok", axis=0, tiled=True),
        lax.all_gather(out_mat, "tok", axis=1, tiled=True),
        lax.all_gather(feed_scale, "tok", axis=0, tiled=True),
        lax.all_gather(gate_mat, "tok", axis=0, tiled=True),
        lax.all_gather(up_mat, "tok", axis=0, tiled=True),
        lax.all_gather(down_mat, "tok", axis=1, tiled=True),
    )
    (
        mix_all,
        branch_all,
        input_all,
        taps_all,
        shift_all,
        rate_all,
        rate_bias,
        entry_all,
        entry_bias,
        logit_all,
        out_all,
        feed_all,
        gate_all,
        up_all,
        down_all,
    ) = fetched
    mix_gain = mix_all.astype(jnp.float32)
    feed_gain = feed_all.astype(jnp.float32)
    tap_values = taps_all.astype(jnp.float32)
    rate_weights = rate_all.astype(jnp.float32)
    entry_weights = entry_all.astype(jnp.float32)
    logit_values = logit_all.astype(jnp.float32)
    channels = branch_all.shape[1]
    groups = rate_all.shape[0]
    width_block = rate_all.shape[1]
    block_ids = jnp.arange(members, dtype=jnp.int32) * tok_total + tok_place
    token_ids = (
        block_ids[:, None] * own_rows + jnp.arange(own_rows, dtype=jnp.int32)[None, :]
    ).reshape(-1)
    item_ends = jnp.cumsum(lengths)
    starts = item_ends - lengths
    opened = jnp.max(jnp.where(starts[None, :] <= token_ids[:, None], starts[None, :], 0), axis=1)
    places = (token_ids - opened).reshape(members, own_rows, 1)
    resets = (places == 0).reshape(-1, 1)
    input_values = inputs.astype(jnp.float32)
    normed_one, factor_one = normalize(input_values, mix_gain)
    wide_one = spread_rows(normed_one.astype(jnp.bfloat16))
    branch = product(wide_one, branch_all)
    gated_branch, branch_pull = jax.vjp(jax.nn.gelu, branch)
    conv_input = product(wide_one, input_all).astype(jnp.bfloat16)
    input_grouped = conv_input.reshape(members, own_rows, channels)
    tail_rows = input_grouped[:, own_rows - (CONV - 1) :]
    arrived = shifted_2(tail_rows, "tok", 1)
    moved_rims = jnp.concatenate([jnp.zeros_like(arrived[:1]), arrived[:-1]], axis=0)
    rim_rows = jnp.where(tok_place == 0, moved_rims, arrived)
    extended = jnp.concatenate([rim_rows, input_grouped], axis=1).astype(jnp.float32)
    tap_masks = [(places >= tap_index).astype(jnp.float32) for tap_index in range(CONV)]
    convolved = shift_all.astype(jnp.float32) + tap_values[0] * input_grouped.astype(jnp.float32)
    for tap_index in range(1, CONV):
        first_row = CONV - 1 - tap_index
        convolved = convolved + tap_values[tap_index] * (
            extended[:, first_row : first_row + own_rows] * tap_masks[tap_index]
        )
    flat_conv = convolved.reshape(-1, channels)
    grouped = flat_conv.reshape(-1, groups, width_block)
    rates = jax.nn.sigmoid(
        jnp.einsum("nhc,hcd->nhd", grouped, rate_weights, precision=highest).reshape(-1, channels)
        + rate_bias.astype(jnp.float32)
    )
    entries = jax.nn.sigmoid(
        jnp.einsum("nhc,hcd->nhd", grouped, entry_weights, precision=highest).reshape(-1, channels)
        + entry_bias.astype(jnp.float32)
    )
    softened = jax.nn.softplus(-logit_values)
    log_keep = -decay_power * softened * rates
    kept_raw = jnp.exp(log_keep)
    keeps = jnp.where(resets, 0.0, kept_raw)
    norm_raw = jnp.sqrt(-jnp.expm1(2.0 * log_keep))
    scaling = jnp.where(resets, 1.0, norm_raw)
    drives = entries * flat_conv * scaling
    keeps_grouped = keeps.reshape(members, own_rows, channels)
    cum_keep, local_state = lax.associative_scan(
        compose, (keeps_grouped, drives.reshape(members, own_rows, channels)), axis=1
    )
    carried = boundary_carry(cum_keep[:, -1], local_state[:, -1], False)
    states_grouped = local_state + cum_keep * carried[:, None, :]
    states = states_grouped.reshape(-1, channels)
    mixture = (states * gated_branch).astype(jnp.bfloat16)
    middle = input_values + settle([(mixture, out_all, False)])
    normed_two, factor_two = normalize(middle, feed_gain)
    wide_two = spread_rows(normed_two.astype(jnp.bfloat16))
    gate_pre = product(wide_two, gate_all)
    up_pre = product(wide_two, up_all)
    gate_act, gate_pull = jax.vjp(jax.nn.gelu, gate_pre)
    hidden = (gate_act * up_pre).astype(jnp.bfloat16)
    layer_out = middle + settle([(hidden, down_all, False)])
    refetched = (
        lax.all_gather(branch_mat, "tok", axis=0, tiled=True),
        lax.all_gather(input_mat, "tok", axis=0, tiled=True),
        lax.all_gather(out_mat, "tok", axis=1, tiled=True),
        lax.all_gather(gate_mat, "tok", axis=0, tiled=True),
        lax.all_gather(up_mat, "tok", axis=0, tiled=True),
        lax.all_gather(down_mat, "tok", axis=1, tiled=True),
    )
    branch_all, input_all, out_all, gate_all, up_all, down_all = refetched
    down_grads = spread_grads(cotangent)
    grad_down = product_outer(hidden, down_grads)
    hidden_grad = product_back(down_grads, down_all)
    gate_grad = gate_pull(hidden_grad * up_pre)[0].astype(jnp.bfloat16)
    up_grad = (hidden_grad * gate_act).astype(jnp.bfloat16)
    grad_gate = product_outer(wide_two, gate_grad)
    grad_up = product_outer(wide_two, up_grad)
    normed_two_grad = settle([(gate_grad, gate_all, True), (up_grad, up_all, True)])
    middle_grad, partial_two = normalize_back(normed_two_grad, middle, factor_two, feed_gain)
    middle_grad = middle_grad + cotangent.astype(jnp.float32)
    middle_wide = spread_grads(middle_grad.astype(jnp.bfloat16))
    grad_out = product_outer(mixture, middle_wide)
    mixture_grad = product_back(middle_wide, out_all)
    states_grad = mixture_grad * gated_branch
    branch_grad = branch_pull(mixture_grad * states)[0].astype(jnp.bfloat16)
    following = jnp.concatenate([keeps_grouped[:, 1:], jnp.ones_like(keeps_grouped[:, :1])], axis=1)
    flipped = lax.associative_scan(
        compose,
        (jnp.flip(following, 1), jnp.flip(states_grad.reshape(members, own_rows, channels), 1)),
        axis=1,
    )
    next_product = jnp.flip(flipped[0], 1)
    local_adjoint = jnp.flip(flipped[1], 1)
    carried_back = boundary_carry(
        keeps_grouped[:, 0] * next_product[:, 0], keeps_grouped[:, 0] * local_adjoint[:, 0], True
    )
    adjoint = (local_adjoint + next_product * carried_back[:, None, :]).reshape(-1, channels)
    previous = jnp.concatenate([carried[:, None, :], states_grouped[:, :-1]], axis=1).reshape(
        -1, channels
    )
    log_grad = jnp.where(
        resets,
        0.0,
        adjoint * previous * kept_raw
        - adjoint * entries * flat_conv * jnp.exp(2.0 * log_keep) / norm_raw,
    )
    grad_logit = jnp.sum(log_grad * rates, axis=0) * decay_power * jax.nn.sigmoid(-logit_values)
    rate_pre_grad = -decay_power * softened * log_grad * rates * (1.0 - rates)
    entry_pre_grad = adjoint * flat_conv * scaling * entries * (1.0 - entries)
    rate_blocks = rate_pre_grad.reshape(-1, groups, width_block)
    entry_blocks = entry_pre_grad.reshape(-1, groups, width_block)
    grad_rate_mat = jnp.einsum("nhc,nhd->hcd", grouped, rate_blocks, precision=highest)
    grad_entry_mat = jnp.einsum("nhc,nhd->hcd", grouped, entry_blocks, precision=highest)
    grad_rate_bias = jnp.sum(rate_pre_grad, axis=0)
    grad_entry_bias = jnp.sum(entry_pre_grad, axis=0)
    gate_back = jnp.einsum(
        "nhd,hcd->nhc", rate_blocks, rate_weights, precision=highest
    ) + jnp.einsum("nhd,hcd->nhc", entry_blocks, entry_weights, precision=highest)
    conv_grad = adjoint * entries * scaling + gate_back.reshape(-1, channels)
    grad_shift = jnp.sum(conv_grad, axis=0)
    conv_grad_grouped = conv_grad.reshape(members, own_rows, channels)
    extended_grad = jnp.zeros_like(extended)
    tap_grads = []
    for tap_index in range(CONV):
        first_row = CONV - 1 - tap_index
        masked = conv_grad_grouped * tap_masks[tap_index]
        tap_grads.append(
            jnp.sum(masked * extended[:, first_row : first_row + own_rows], axis=(0, 1))
        )
        extended_grad = extended_grad + jnp.pad(
            tap_values[tap_index] * masked, ((0, 0), (first_row, CONV - 1 - first_row), (0, 0))
        )
    grad_taps = jnp.stack(tap_grads)
    returned = shifted_2(extended_grad[:, : CONV - 1], "tok", -1)
    moved_back = jnp.concatenate([returned[1:], jnp.zeros_like(returned[:1])], axis=0)
    landing = jnp.where(tok_place == tok_total - 1, moved_back, returned)
    input_grad = extended_grad[:, CONV - 1 :] + jnp.pad(
        landing, ((0, 0), (own_rows - (CONV - 1), 0), (0, 0))
    )
    input_low = input_grad.reshape(-1, channels).astype(jnp.bfloat16)
    grad_input = product_outer(wide_one, input_low)
    grad_branch = product_outer(wide_one, branch_grad)
    normed_one_grad = settle([(branch_grad, branch_all, True), (input_low, input_all, True)])
    first_grad, partial_one = normalize_back(normed_one_grad, input_values, factor_one, mix_gain)
    inputs_grad = (middle_grad + first_grad).astype(jnp.bfloat16)
    partial_one, partial_two = lax.psum((partial_one, partial_two), "blk")
    gradients = (
        lax.psum_scatter(
            partial_one.astype(jnp.bfloat16), "tok", scatter_dimension=0, tiled=True
        ).astype(jnp.float32),
        lax.psum_scatter(
            grad_branch.astype(jnp.bfloat16), "tok", scatter_dimension=0, tiled=True
        ).astype(jnp.float32),
        lax.psum_scatter(
            grad_input.astype(jnp.bfloat16), "tok", scatter_dimension=0, tiled=True
        ).astype(jnp.float32),
        lax.psum_scatter(
            grad_taps.astype(jnp.bfloat16), "tok", scatter_dimension=1, tiled=True
        ).astype(jnp.float32),
        lax.psum_scatter(
            grad_shift.astype(jnp.bfloat16), "tok", scatter_dimension=0, tiled=True
        ).astype(jnp.float32),
        lax.psum_scatter(
            grad_rate_mat.astype(jnp.bfloat16), "tok", scatter_dimension=1, tiled=True
        ).astype(jnp.float32),
        lax.psum_scatter(
            grad_rate_bias.astype(jnp.bfloat16), "tok", scatter_dimension=0, tiled=True
        ).astype(jnp.float32),
        lax.psum_scatter(
            grad_entry_mat.astype(jnp.bfloat16), "tok", scatter_dimension=1, tiled=True
        ).astype(jnp.float32),
        lax.psum_scatter(
            grad_entry_bias.astype(jnp.bfloat16), "tok", scatter_dimension=0, tiled=True
        ).astype(jnp.float32),
        lax.psum_scatter(
            grad_logit.astype(jnp.bfloat16), "tok", scatter_dimension=0, tiled=True
        ).astype(jnp.float32),
        lax.psum_scatter(
            grad_out.astype(jnp.bfloat16), "tok", scatter_dimension=1, tiled=True
        ).astype(jnp.float32),
        lax.psum_scatter(
            partial_two.astype(jnp.bfloat16), "tok", scatter_dimension=0, tiled=True
        ).astype(jnp.float32),
        lax.psum_scatter(
            grad_gate.astype(jnp.bfloat16), "tok", scatter_dimension=0, tiled=True
        ).astype(jnp.float32),
        lax.psum_scatter(
            grad_up.astype(jnp.bfloat16), "tok", scatter_dimension=0, tiled=True
        ).astype(jnp.float32),
        lax.psum_scatter(
            grad_down.astype(jnp.bfloat16), "tok", scatter_dimension=1, tiled=True
        ).astype(jnp.float32),
    )
    return (layer_out.astype(jnp.bfloat16), inputs_grad) + tuple(gradients)


def solution(mesh):
    in_specs = (
        P(("blk", "tok"), None),
        P("tok"),
        P("tok", "blk"),
        P("tok", "blk"),
        P(None, ("blk", "tok")),
        P(("blk", "tok")),
        P("blk", "tok", None),
        P(("blk", "tok")),
        P("blk", "tok", None),
        P(("blk", "tok")),
        P(("blk", "tok")),
        P("blk", "tok"),
        P("tok"),
        P("tok", "blk"),
        P("tok", "blk"),
        P("blk", "tok"),
        P(),
        P(("blk", "tok"), None),
    )
    out_specs = (
        P(("blk", "tok"), None),
        P(("blk", "tok"), None),
        P("tok"),
        P("tok", "blk"),
        P("tok", "blk"),
        P(None, ("blk", "tok")),
        P(("blk", "tok")),
        P("blk", "tok", None),
        P(("blk", "tok")),
        P("blk", "tok", None),
        P(("blk", "tok")),
        P(("blk", "tok")),
        P("blk", "tok"),
        P("tok"),
        P("tok", "blk"),
        P("tok", "blk"),
        P("blk", "tok"),
    )
    return jax.shard_map(
        per_device, mesh=mesh, in_specs=in_specs, out_specs=out_specs, check_vma=False
    )
```

profile of v0, /device:TPU:0, one launch (start us, length us, event | category | flops | bytes accessed | tf_op | source)
XLA Modules:
  0.0 1727.6 jit_solution(16422466632757686610)
XLA Ops:
  14.9 129.8 %all-reduce.112 = (bf16[640]{0:T(1024)(128)(2,1)S(1)}, bf16[2048]{0:T(1024)(128)(2,1)S(1)}, bf16[640]{0:T(1024)(128)(2,1)S(1)}, bf16[640]{0:T(1024)(128)(2,1)S(1...) all-reduce(bf16[640]{0:T(1024)(128)(2,1)S(1)} %dynamic-update-slice, ...), channel_id=1, replica_groups=mesh['blk'=4,'tok'=32] {'tok'}, use_global_device_ids=true, to_apply=%add.98 | all-reduce | flops 6656 | bytes 26624
  152.4 20.5 %all-gather.4 = bf16[32,20,4]{1,2,0:T(4,128)(2,1)S(1)} all-gather(bf16[1,20,4]{1,2,0:T(4,128)(2,1)S(1)} %bitcast.205), channel_id=1, replica_groups=mesh['blk'=4,'tok'=32] {'tok'}, dimensions={0}, use_global_device_ids=true | all-gather | bytes 5280 | tf_op jit(solution)/shard_map/all_gather | solution.py:119
  173.3 25.6 %all_gather.80 = bf16[4,160,160]{2,0,1:T(4,128)(2,1)S(1)} all-gather(bf16[4,5,160]{2,0,1:T(4,128)(2,1)S(1)} %copy-done.105), channel_id=1, replica_groups=mesh['blk'=4,'tok'=32] {'tok'}, dimensions={1}, use_global_device_ids=true | all-gather | bytes 211200 | tf_op jit(solution)/shard_map/all_gather | solution.py:123
  199.0 23.9 %all-gather.18.cloned.1.call-done = bf16[2048,640]{1,0:T(8,128)(2,1)} async-done(((bf16[64,640]{1,0:T(8,128)(2,1)}), bf16[2048,640]{1,0:T(8,128)(2,1)}) %all-gather.18.cloned.1.call-update) | async-done | bytes 2621456 | tf_op jit(solution)/shard_map/all_gather | solution.py:118
  222.9 4.2 convolution_convert_fusion.6
  227.4 24.3 %all_gather.83 = bf16[4,160,160]{2,0,1:T(4,128)(2,1)S(1)} all-gather(bf16[4,5,160]{2,0,1:T(4,128)(2,1)S(1)} %copy-done.106), channel_id=1, replica_groups=mesh['blk'=4,'tok'=32] {'tok'}, dimensions={1}, use_global_device_ids=true | all-gather | bytes 211200 | tf_op jit(solution)/shard_map/all_gather | solution.py:121
  271.8 4.4 multiply_multiply_fusion.5
  276.2 3.5 slice.839
  355.7 3.6 pad.293
  360.0 3.6 pad.292
  369.7 4.1 pad.309
  375.8 4.4 pad.311
  383.9 4.0 pad.295
  391.8 4.5 pad.310
  397.2 25.5 %all-gather.1 = f32[128,1,640]{2,1,0:T(1,128)} all-gather(f32[4,1,640]{2,1,0:T(1,128)S(1)} %slice_add_fusion.3), channel_id=3, replica_groups=mesh['blk'=4,'tok'=32] {'tok'}, dimensions={0}, use_global_device_ids=true | all-gather | bytes 337920 | tf_op jit(solution)/shard_map/all_gather | solution.py:74
  436.6 4.5 pad.296
  441.9 23.8 %all-gather = f32[128,1,640]{2,1,0:T(1,128)S(1)} all-gather(f32[4,1,640]{2,1,0:T(1,128)S(1)} %slice_add_fusion.4), channel_id=2, replica_groups=mesh['blk'=4,'tok'=32] {'tok'}, dimensions={0}, use_global_device_ids=true | all-gather | bytes 337920 | tf_op jit(solution)/shard_map/all_gather | solution.py:75
  470.4 3.4 multiply_add_fusion.2
  473.8 5.7 fusion.17
  479.5 5.8 fusion.104
  485.9 44.6 %reduce-scatter.12.cloned.1.call-done = f32[128,2048]{1,0:T(8,128)} async-done(((f32[512,2048]{1,0:T(8,128)}), f32[128,2048]{1,0:T(8,128)}) %reduce-scatter.12.cloned.1.call-update) | async-done | bytes 1048592 | tf_op jit(solution)/shard_map/reduce_scatter | solution.py:69
  535.3 46.7 %all-gather.26.cloned.1.call-done = bf16[2048,1536]{1,0:T(8,128)(2,1)} async-done(((bf16[64,1536]{1,0:T(8,128)(2,1)}), bf16[2048,1536]{1,0:T(8,128)(2,1)}) %all-gather.26.cloned.1.call-update) | async-done | bytes 6291472 | tf_op jit(solution)/shard_map/all_gather | solution.py:128
  582.0 32.0 %all-gather.24.cloned.1.call-done = bf16[512,2048]{1,0:T(8,128)(2,1)} async-done(((bf16[128,2048]{1,0:T(8,128)(2,1)}), bf16[512,2048]{1,0:T(8,128)(2,1)}) %all-gather.24.cloned.1.call-update) | async-done | bytes 2097168 | tf_op jit(solution)/shard_map/all_gather | solution.py:55
  614.0 8.5 fusion.105
  622.5 43.4 %all-gather.28.cloned.1.call-done = bf16[2048,1536]{1,0:T(8,128)(2,1)} async-done(((bf16[64,1536]{1,0:T(8,128)(2,1)}), bf16[2048,1536]{1,0:T(8,128)(2,1)}) %all-gather.28.cloned.1.call-update) | async-done | bytes 6291472 | tf_op jit(solution)/shard_map/all_gather | solution.py:129
  665.9 8.6 fusion.106
  674.5 22.8 %all-gather.32.cloned.1.call-done = bf16[512,2048]{1,0:T(8,128)(2,1)} async-done(((bf16[128,2048]{1,0:T(8,128)(2,1)}), bf16[512,2048]{1,0:T(8,128)(2,1)}) %all-gather.32.cloned.1.call-update) | async-done | bytes 2097168 | tf_op jit(solution)/shard_map/all_gather | solution.py:59
  697.3 51.7 %all-gather.30.cloned.1.call-done = bf16[1536,2048]{0,1:T(8,128)(2,1)} async-done(((bf16[1536,64]{0,1:T(8,128)(2,1)}), bf16[1536,2048]{0,1:T(8,128)(2,1)}) %all-gather.30.cloned.1.call-update) | async-done | bytes 6291472 | tf_op jit(solution)/shard_map/all_gather | solution.py:130
  749.1 11.7 multiply_convert_fusion
  760.8 6.7 fusion.108
  767.6 5.0 convolution_add_fusion.1
  772.8 8.8 fusion.107
  781.7 36.6 %reduce-scatter.16.cloned.1.call-done = f32[128,2048]{1,0:T(8,128)} async-done(((f32[512,2048]{1,0:T(8,128)}), f32[128,2048]{1,0:T(8,128)}) %reduce-scatter.16.cloned.1.call-update) | async-done | bytes 1048592 | tf_op jit(solution)/shard_map/reduce_scatter | solution.py:69
  820.5 46.6 %reduce-scatter.14.cloned.1.call-done = f32[128,2048]{1,0:T(8,128)} async-done(((f32[512,2048]{1,0:T(8,128)}), f32[128,2048]{1,0:T(8,128)}) %reduce-scatter.14.cloned.1.call-update) | async-done | bytes 1048592 | tf_op jit(solution)/shard_map/reduce_scatter | solution.py:69
  870.3 8.1 convolution_convert_fusion.2
  880.2 6.9 convolution_convert_fusion.1
  893.3 3.7 slice.961
  901.9 8.1 convolution_convert_fusion
  911.3 6.6 fusion.30
  917.9 3.5 slice.957
  921.7 3.6 slice.958
  990.6 4.0 pad.337
  996.6 4.5 pad.339
  1001.1 3.7 slice.1013
  1014.0 25.0 %all-gather.2 = f32[128,1,640]{2,1,0:T(1,128)S(1)} all-gather(f32[4,1,640]{2,1,0:T(1,128)S(1)} %get-tuple-element.111), channel_id=4, replica_groups=mesh['blk'=4,'tok'=32] {'tok'}, dimensions={0}, use_global_device_ids=true | all-gather | bytes 337920 | tf_op jit(solution)/shard_map/all_gather | solution.py:75
  1040.2 24.6 %all-gather.3 = f32[128,1,640]{2,1,0:T(1,128)S(1)} all-gather(f32[4,1,640]{2,1,0:T(1,128)S(1)} %get-tuple-element.110), channel_id=5, replica_groups=mesh['blk'=4,'tok'=32] {'tok'}, dimensions={0}, use_global_device_ids=true | all-gather | bytes 337920 | tf_op jit(solution)/shard_map/all_gather | solution.py:74
  1074.2 6.5 rev.16
  1080.8 10.9 rev.15
  1091.8 4.7 subtract_select_fusion
  1106.3 4.2 subtract_multiply_fusion
  1115.4 5.0 convolution_convert_fusion.3
  1121.5 5.0 convolution_convert_fusion.5
  1129.6 4.2 add_reduce_fusion
  1138.0 5.0 multiply_reduce_fusion
  1152.9 3.7 fusion.109
  1156.7 3.8 convolution_add_fusion
  1166.0 4.9 reduce-scatter.30.cloned.1.call-done
  1172.8 104.4 %all-reduce.116.cloned.1.call-done = (bf16[4,160,160]{2,0,1:T(4,128)(2,1)}, bf16[4,160,160]{2,0,1:T(4,128)(2,1)}) async-done(((bf16[4,160,160]{2,0,1:T(4,128)(2,1)}, bf16[4,160,160]{2,0,1:T(4,128)(2,1)}), (bf16[4,160,160]{2,0,1:T(4,128)(2,1)}, bf16[4,160,160]{2,0,1:T(4,128)(2,1)})) %all-reduce.116.cloned.1.call-update) | async-done | bytes 409616
  1279.7 79.9 %reduce-scatter.24.cloned.1.call-done = bf16[640,64]{0,1:T(8,128)(2,1)} async-done(((bf16[640,2048]{0,1:T(8,128)(2,1)}), bf16[640,64]{0,1:T(8,128)(2,1)}) %reduce-scatter.24.cloned.1.call-update) | async-done | bytes 81936 | tf_op jit(solution)/shard_map/reduce_scatter | solution.py:335
  1361.2 81.3 %reduce-scatter.20.cloned.1.call-done = bf16[64,640]{1,0:T(8,128)(2,1)} async-done(((bf16[2048,640]{1,0:T(8,128)(2,1)}), bf16[64,640]{1,0:T(8,128)(2,1)}) %reduce-scatter.20.cloned.1.call-update) | async-done | bytes 81936 | tf_op jit(solution)/shard_map/reduce_scatter | solution.py:308
  1444.0 80.6 %reduce-scatter.22.cloned.1.call-done = bf16[64,640]{1,0:T(8,128)(2,1)} async-done(((bf16[2048,640]{1,0:T(8,128)(2,1)}), bf16[64,640]{1,0:T(8,128)(2,1)}) %reduce-scatter.22.cloned.1.call-update) | async-done | bytes 81936 | tf_op jit(solution)/shard_map/reduce_scatter | solution.py:311
  1526.2 47.0 %reduce-scatter.18.cloned.1.call-done = f32[128,2048]{1,0:T(8,128)} async-done(((f32[512,2048]{1,0:T(8,128)}), f32[128,2048]{1,0:T(8,128)}) %reduce-scatter.18.cloned.1.call-update) | async-done | bytes 1048592 | tf_op jit(solution)/shard_map/reduce_scatter | solution.py:69
  1574.9 15.0 all-reduce.110
  1589.9 125.0 %all-reduce.111 = (bf16[2048]{0:T(1024)(128)(2,1)S(1)}, bf16[4,640]{1,0:T(4,128)(2,1)S(1)}, bf16[640]{0:T(1024)(128)(2,1)S(1)}, bf16[640]{0:T(1024)(128)(2,1)S(1...) all-reduce(bf16[2048]{0:T(1024)(128)(2,1)S(1)} %get-tuple-element.6, ...), channel_id=10, replica_groups=mesh['blk'=4,'tok'=32] {'tok'}, use_global_device_ids=true, to_apply=%region_12.14.clone | all-reduce | flops 9216 | bytes 36864
  (812 shorter events, 310.6 us)
Async XLA Ops:
  7.2 144.2 %copy-start.129 = (s32[5]{0:T(128)S(1)}, s32[5]{0:T(128)}, u32[]{:S(2)}) copy-start(s32[5]{0:T(128)} %param.36) | copy-start | bytes 64
  7.2 145.2 %copy-start.124 = (bf16[4,20]{1,0:T(4,128)(2,1)S(1)}, bf16[4,20]{1,0:T(4,128)(2,1)}, u32[]{:S(2)}) copy-start(bf16[4,20]{1,0:T(4,128)(2,1)} %param.24) | copy-start | bytes 484
  7.2 191.8 %all-gather.16.cloned.1.call-start = ((), (), s32[]{:S(2)}) async-start(), calls=%async_computation.10 | async-start | bytes 2621440 | tf_op jit(solution)/shard_map/all_gather | solution.py:55
  144.7 54.2 %copy-start.113 = (bf16[640]{0:T(1024)(128)(2,1)}, bf16[640]{0:T(1024)(128)(2,1)S(1)}, u32[]{:S(2)}) copy-start(bf16[640]{0:T(1024)(128)(2,1)S(1)} %get-tuple-element.76) | copy-start | bytes 3844
  144.8 107.0 %copy-start.109 = (bf16[640]{0:T(1024)(128)(2,1)}, bf16[640]{0:T(1024)(128)(2,1)S(1)}, u32[]{:S(2)}) copy-start(bf16[640]{0:T(1024)(128)(2,1)S(1)} %get-tuple-element.80) | copy-start | bytes 3844
  144.8 107.0 %copy-start.111 = (bf16[640]{0:T(1024)(128)(2,1)}, bf16[640]{0:T(1024)(128)(2,1)S(1)}, u32[]{:S(2)}) copy-start(bf16[640]{0:T(1024)(128)(2,1)S(1)} %get-tuple-element.79) | copy-start | bytes 3844
  144.8 28.1 %copy-start.54 = (f32[2048]{0:T(1024)}, f32[2048]{0:T(1024)S(1)}, u32[]{:S(2)}) copy-start(f32[2048]{0:T(1024)S(1)} %convert_element_type.210) | copy-start | bytes 24580
  144.8 28.5 %copy-start.105 = (bf16[4,5,160]{2,0,1:T(4,128)(2,1)S(1)}, bf16[4,5,160]{2,0,1:T(4,128)(2,1)}, u32[]{:S(2)}) copy-start(bf16[4,5,160]{2,0,1:T(4,128)(2,1)} %param.28) | copy-start | bytes 19204
  148.7 74.2 %all-gather.18.cloned.1.call-start = ((), (), s32[]{:S(2)}) async-start(), calls=%async_computation.11 | async-start | bytes 2703360 | tf_op jit(solution)/shard_map/all_gather | solution.py:118
  149.4 324.4 %all-gather.20.cloned.1.call-start = ((), (), s32[]{:S(2)}) async-start(), calls=%async_computation.12 | async-start | bytes 2703360 | tf_op jit(solution)/shard_map/all_gather | solution.py:117
  150.2 329.3 %all-gather.22.cloned.1.call-start = ((), (), s32[]{:S(2)}) async-start(), calls=%async_computation.13 | async-start | bytes 2703360 | tf_op jit(solution)/shard_map/all_gather | solution.py:126
  150.7 379.8 %reduce-scatter.12.cloned.1.call-start = ((), (), s32[]{:S(2)}) async-start(), calls=%async_computation.14 | async-start | bytes 5242880 | tf_op jit(solution)/shard_map/reduce_scatter | solution.py:69
  150.8 76.2 %copy-start.118 = (s32[4]{0:T(128)}, s32[4]{0:T(128)S(1)}, u32[]{:S(2)}) copy-start(s32[4]{0:T(128)S(1)} %fusion.81) | copy-start | bytes 52
  152.4 99.6 %copy-start.95 = (f32[4,128]{1,0:T(4,128)}, f32[4,128]{1,0:T(4,128)S(1)}, u32[]{:S(2)}) copy-start(f32[4,128]{1,0:T(4,128)S(1)} %get-tuple-element.202) | copy-start | bytes 6148
  152.4 99.6 %copy-start.97 = (f32[4,128]{1,0:T(4,128)}, f32[4,128]{1,0:T(4,128)S(1)}, u32[]{:S(2)}) copy-start(f32[4,128]{1,0:T(4,128)S(1)} %get-tuple-element.203) | copy-start | bytes 6148
  152.4 99.7 %copy-start.99 = (f32[4,128]{1,0:T(4,128)}, f32[4,128]{1,0:T(4,128)S(1)}, u32[]{:S(2)}) copy-start(f32[4,128]{1,0:T(4,128)S(1)} %get-tuple-element.205) | copy-start | bytes 6148
  152.4 119.4 %copy-start.107 = (pred[4,128]{1,0:T(4,128)(4,1)}, pred[4,128]{1,0:T(4,128)(4,1)S(1)}, u32[]{:S(2)}) copy-start(pred[4,128]{1,0:T(4,128)(4,1)S(1)} %get-tuple-element.204) | copy-start | bytes 1540
  173.3 78.7 %copy-start.87 = (f32[640]{0:T(1024)}, f32[640]{0:T(1024)S(1)}, u32[]{:S(2)}) copy-start(f32[640]{0:T(1024)S(1)} %get-tuple-element.63) | copy-start | bytes 7684
  173.3 78.7 %copy-start.89 = (f32[640]{0:T(1024)}, f32[640]{0:T(1024)S(1)}, u32[]{:S(2)}) copy-start(f32[640]{0:T(1024)S(1)} %get-tuple-element.64) | copy-start | bytes 7684
  173.3 78.7 %copy-start.91 = (f32[640]{0:T(1024)}, f32[640]{0:T(1024)S(1)}, u32[]{:S(2)}) copy-start(f32[640]{0:T(1024)S(1)} %get-tuple-element.65) | copy-start | bytes 7684
  173.3 78.7 %copy-start.93 = (f32[640]{0:T(1024)}, f32[640]{0:T(1024)S(1)}, u32[]{:S(2)}) copy-start(f32[640]{0:T(1024)S(1)} %get-tuple-element.66) | copy-start | bytes 7684
  198.9 58.5 %copy-start.42 = (bf16[4,160,160]{2,0,1:T(4,128)(2,1)}, bf16[4,160,160]{2,0,1:T(4,128)(2,1)S(1)}, u32[]{:S(2)}) copy-start(bf16[4,160,160]{2,0,1:T(4,128)(2,1)S(1)} %all_gather.80) | copy-start | bytes 614404
  198.9 270.3 %copy-start.115 = (s32[1024]{0:T(1024)}, s32[1024]{0:T(1024)S(1)}, u32[]{:S(2)}) copy-start(s32[1024]{0:T(1024)S(1)} %pad_clamp_fusion) | copy-start | bytes 12292
  199.0 28.4 %copy-start.106 = (bf16[4,5,160]{2,0,1:T(4,128)(2,1)S(1)}, bf16[4,5,160]{2,0,1:T(4,128)(2,1)}, u32[]{:S(2)}) copy-start(bf16[4,5,160]{2,0,1:T(4,128)(2,1)} %param.26) | copy-start | bytes 19204
  227.1 24.7 %collective-permute-start = (bf16[4,3,640]{2,1,0:T(4,128)(2,1)S(1)}, bf16[4,3,640]{2,1,0:T(4,128)(2,1)S(1)}, u32[]{:S(2)}, u32[]{:S(2)}) collective-permute-start(bf16[4,3,640]{2,1,0:T(4,128)(2,1)S(1)} %slice.1097), channel_id=1, source_target_pairs={{31,0},{0,1},{1,2},{2,3},{3,4},{4,5},{5,6},{6,7},{7,8},{8,9},{9,10... | collective-permute-start | bytes 46088 | tf_op jit(solution)/shard_map/ppermute | solution.py:17
  251.7 12.8 copy-start.32
  251.7 20.0 %copy-start.59 = (f32[640]{0:T(1024)}, f32[640]{0:T(1024)S(1)}, u32[]{:S(2)}) copy-start(f32[640]{0:T(1024)S(1)} %convert_element_type.218) | copy-start | bytes 7684
  251.8 20.0 %copy-start.61 = (f32[640]{0:T(1024)}, f32[640]{0:T(1024)S(1)}, u32[]{:S(2)}) copy-start(f32[640]{0:T(1024)S(1)} %convert_element_type.220) | copy-start | bytes 7684
  253.9 17.8 %copy-start.4 = (f32[4,128,640]{2,1,0:T(8,128)}, f32[4,128,640]{2,1,0:T(8,128)S(1)}, u32[]{:S(2)}) copy-start(f32[4,128,640]{2,1,0:T(8,128)S(1)} %multiply_add_fusion.3) | copy-start | bytes 3932164
  257.5 7.1 copy-start.2
  485.3 45.3 %copy-start.9 = (bf16[128,2048]{1,0:T(8,128)(2,1)S(1)}, bf16[128,2048]{1,0:T(8,128)(2,1)}, u32[]{:S(2)}) copy-start(bf16[128,2048]{1,0:T(8,128)(2,1)} %param.20) | copy-start | bytes 1572868
  485.3 96.7 %all-gather.26.cloned.1.call-start = ((), (), s32[]{:S(2)}) async-start(), calls=%async_computation.16 | async-start | bytes 6488064 | tf_op jit(solution)/shard_map/all_gather | solution.py:128
  485.9 128.1 %all-gather.24.cloned.1.call-start = ((), (), s32[]{:S(2)}) async-start(), calls=%async_computation.15 | async-start | bytes 2621440 | tf_op jit(solution)/shard_map/all_gather | solution.py:55
  533.0 132.9 %all-gather.28.cloned.1.call-start = ((), (), s32[]{:S(2)}) async-start(), calls=%async_computation.17 | async-start | bytes 6488064 | tf_op jit(solution)/shard_map/all_gather | solution.py:129
  533.8 163.6 %all-gather.32.cloned.1.call-start = ((), (), s32[]{:S(2)}) async-start(), calls=%async_computation.20 | async-start | bytes 2621440 | tf_op jit(solution)/shard_map/all_gather | solution.py:59
  534.5 214.6 %all-gather.30.cloned.1.call-start = ((), (), s32[]{:S(2)}) async-start(), calls=%async_computation.18 | async-start | bytes 6488064 | tf_op jit(solution)/shard_map/all_gather | solution.py:130
  535.1 283.2 %reduce-scatter.16.cloned.1.call-start = ((), (), s32[]{:S(2)}) async-start(), calls=%async_computation.21 | async-start | bytes 5242880 | tf_op jit(solution)/shard_map/reduce_scatter | solution.py:69
  772.6 94.5 %reduce-scatter.14.cloned.1.call-start = ((), (), s32[]{:S(2)}) async-start(), calls=%async_computation.19 | async-start | bytes 5242880 | tf_op jit(solution)/shard_map/reduce_scatter | solution.py:69
  781.6 128.8 %all-gather.34.cloned.1.call-start = ((), (), s32[]{:S(2)}) async-start(), calls=%async_computation.22 | async-start | bytes 2621440 | tf_op jit(solution)/shard_map/all_gather | solution.py:59
  818.3 48.8 %copy-start.27 = (f32[128,2048]{1,0:T(8,128)S(1)}, f32[128,2048]{1,0:T(8,128)}, u32[]{:S(2)}) copy-start(f32[128,2048]{1,0:T(8,128)} %reduce-scatter.16.cloned.1.call-done) | copy-start | bytes 3145732
  870.3 292.3 %reduce-scatter.26.cloned.1.call-start = ((), (), s32[]{:S(2)}) async-start(), calls=%async_computation.27 | async-start | bytes 6488064 | tf_op jit(solution)/shard_map/reduce_scatter | solution.py:341
  878.5 285.8 %reduce-scatter.28.cloned.1.call-start = ((), (), s32[]{:S(2)}) async-start(), calls=%async_computation.28 | async-start | bytes 6488064 | tf_op jit(solution)/shard_map/reduce_scatter | solution.py:344
  887.1 283.7 %reduce-scatter.30.cloned.1.call-start = ((), (), s32[]{:S(2)}) async-start(), calls=%async_computation.29 | async-start | bytes 6488064 | tf_op jit(solution)/shard_map/reduce_scatter | solution.py:347
  910.0 367.1 %all-reduce.116.cloned.1.call-start = ((), (), s32[]{:S(2)}) async-start(), calls=%async_computation.30 | async-start | bytes 1310720
  1072.8 18.8 %copy-start.121 = (pred[4]{0:T(512)(128)(4,1)S(1)}, pred[4]{0:T(512)(128)(4,1)}, u32[]{:S(2)}) copy-start(pred[4]{0:T(512)(128)(4,1)} %compare_and_fusion) | copy-start | bytes 16
  1080.7 11.0 copy-start.5
  1080.8 11.0 copy-start.7
  1080.8 11.0 copy-start.60
  1080.8 11.0 copy-start.62
  1080.8 11.0 copy-start.63
  1080.8 11.0 copy-start.108
  1115.3 244.3 %reduce-scatter.24.cloned.1.call-start = ((), (), s32[]{:S(2)}) async-start(), calls=%async_computation.26 | async-start | bytes 2703360 | tf_op jit(solution)/shard_map/reduce_scatter | solution.py:335
  1120.4 322.1 %reduce-scatter.20.cloned.1.call-start = ((), (), s32[]{:S(2)}) async-start(), calls=%async_computation.24 | async-start | bytes 2703360 | tf_op jit(solution)/shard_map/reduce_scatter | solution.py:308
  1126.5 398.2 %reduce-scatter.22.cloned.1.call-start = ((), (), s32[]{:S(2)}) async-start(), calls=%async_computation.25 | async-start | bytes 2703360 | tf_op jit(solution)/shard_map/reduce_scatter | solution.py:311
  1143.6 4.5 collective-permute-start.1
  1151.9 421.4 %reduce-scatter.18.cloned.1.call-start = ((), (), s32[]{:S(2)}) async-start(), calls=%async_computation.23 | async-start | bytes 5242880 | tf_op jit(solution)/shard_map/reduce_scatter | solution.py:69
  1160.5 12.2 copy-start.114
  1162.5 410.8 %copy-start.10 = (bf16[128,2048]{1,0:T(8,128)(2,1)S(1)}, bf16[128,2048]{1,0:T(8,128)(2,1)}, u32[]{:S(2)}) copy-start(bf16[128,2048]{1,0:T(8,128)(2,1)} %param.20) | copy-start | bytes 1572868
  1162.5 410.8 %copy-start.55 = (f32[2048]{0:T(1024)S(1)}, f32[2048]{0:T(1024)}, u32[]{:S(2)}) copy-start(f32[2048]{0:T(1024)} %copy-done.54) | copy-start | bytes 24580
  1162.5 410.8 %copy-start.117 = (f32[128]{0:T(128)S(1)}, f32[128]{0:T(128)}, u32[]{:S(2)}) copy-start(f32[128]{0:T(128)} %copy-done.116) | copy-start | bytes 1540
  1172.6 402.3 %copy-start.101 = (f32[2048]{0:T(1024)S(1)}, f32[2048]{0:T(1024)}, u32[]{:S(2)}) copy-start(f32[2048]{0:T(1024)} %get-tuple-element.58) | copy-start | bytes 24580
  1172.6 546.5 %copy-start.26 = (f32[128,2048]{1,0:T(8,128)S(1)}, f32[128,2048]{1,0:T(8,128)}, u32[]{:S(2)}) copy-start(f32[128,2048]{1,0:T(8,128)} %get-tuple-element.89) | copy-start | bytes 3145732
  1172.6 546.5 %copy-start.125 = (f32[128]{0:T(128)S(1)}, f32[128]{0:T(128)}, u32[]{:S(2)}) copy-start(f32[128]{0:T(128)} %get-tuple-element.208) | copy-start | bytes 1540
  1573.3 145.8 %copy-start.28 = (f32[128,2048]{1,0:T(8,128)S(1)}, f32[128,2048]{1,0:T(8,128)}, u32[]{:S(2)}) copy-start(f32[128,2048]{1,0:T(8,128)} %reduce-scatter.18.cloned.1.call-done) | copy-start | bytes 3145732
  (95 other events, 296.2 us)
Sparse Core Ops, SparseCore 0:
  148.8 27.0 all-gather.15
  178.2 44.6 all-gather.17
  225.1 43.8 all-gather.19
  271.1 43.8 all-gather.21
  485.4 45.1 reduce-scatter.11
  532.9 49.0 all-gather.25
  584.3 29.6 all-gather.23
  616.5 49.3 all-gather.27
  667.7 29.6 all-gather.31
  699.7 49.3 all-gather.29
  772.7 45.5 reduce-scatter.15
  820.6 46.4 reduce-scatter.13
  870.4 30.5 all-gather.33
  905.0 86.4 reduce-scatter.25
  995.1 85.8 reduce-scatter.27
  1085.1 85.7 reduce-scatter.29
  1174.6 102.4 all-reduce.115
  1280.5 79.0 reduce-scatter.23
  1363.6 78.7 reduce-scatter.19
  1445.9 78.7 reduce-scatter.21
  1527.2 46.0 reduce-scatter.17
where the time goes:
time: 1740 us; the launch traced here: 1730 us
  waiting for transfers between devices  752 us (43%)
  blocking collectives  439 us (25%)
  local copies, waits for them, and re-layouts  257 us (15%)
  matrix products  127 us (7%)
  other arithmetic  126 us (7%)
  between operations  20.8 us (1%)
    unnamed x2, blocking collectives  255 us
    reduce_scatter x4, waiting for transfers between devices, settle(): return lax.psum_scatter(running, 'blk', scatter_dimension=0, tiled=True)  175 us
    unnamed x22, waiting for transfers between devices  109 us
    reduce_scatter x1, waiting for transfers between devices, per_device(): lax.psum_scatter(grad_branch.astype(jnp.bfloat16), 'tok', scatter_dimensi...  81.3 us
    reduce_scatter x1, waiting for transfers between devices, per_device(): lax.psum_scatter(grad_input.astype(jnp.bfloat16), 'tok', scatter_dimensio...  80.6 us
    reduce_scatter x1, waiting for transfers between devices, per_device(): lax.psum_scatter(grad_out.astype(jnp.bfloat16), 'tok', scatter_dimension=...  79.9 us
    slice x49, local copies, waits for them, and re-layouts, per_device(): lax.associative_scan(compose, (jnp.flip(following, 1), jnp.flip(states_gr...  60.8 us
    slice x44, local copies, waits for them, and re-layouts, per_device(): lax.associative_scan(compose, (keeps_grouped, drives.reshape(members, own...  55.8 us
  transfers between devices with their start and end apart: 23, of which 16 were waited for; matrix products, arithmetic and copies ran while one was open for 26% of the time, Pallas kernels for 0%

commit v1 on v0

v1 whole, which is shorter than its diff:
```python
import jax
import jax.numpy as jnp
from jax import lax
from jax.experimental import pallas as pl
from jax.experimental.pallas import tpu as pltpu
from jax.sharding import PartitionSpec as P

CONV = 4
MEMBERS = 4
TOKS = 32
OWN = 128
HALO = 16

eps_norm = 1e-06
decay_power = 8.0
f32 = jnp.float32
bf16 = jnp.bfloat16


def hop_blk(values, distance):
    return lax.ppermute(
        values, "blk", [(i, (i + distance) % MEMBERS) for i in range(MEMBERS)]
    )


def hop_tok(values, axis, distance):
    route = []
    for y in range(4):
        for z in range(4):
            for c in range(2):
                if axis == "y":
                    to = ((y + distance) % 4, z, c)
                elif axis == "z":
                    to = (y, (z + distance) % 4, c)
                else:
                    to = (y, z, (c + distance) % 2)
                route.append((y * 8 + z * 2 + c, to[0] * 8 + to[1] * 2 + to[2]))
    return lax.ppermute(values, "tok", route)


def hop(values, axis, distance):
    if axis == "blk":
        return hop_blk(values, distance)
    return hop_tok(values, axis, distance)


def ring_gather(values, axis="blk"):
    half = values.shape[0] // 2
    before = hop(values, axis, 1)
    after = hop(values, axis, -1)
    far_head = hop(before[:half], axis, 1)
    far_tail = hop(after[half:], axis, -1)
    return [values, after, jnp.concatenate([far_head, far_tail]), before]


def narrow_sum(left, right):
    return (left.astype(f32) + right.astype(f32)).astype(bf16)


def ring_scatter(parts, axis="blk"):
    half = parts[2].shape[0] // 2
    head = hop(parts[2][:half].astype(bf16), axis, 1)
    tail = hop(parts[2][half:].astype(bf16), axis, -1)
    forth = jnp.concatenate([narrow_sum(parts[1][:half], head), parts[1][half:].astype(bf16)])
    back = jnp.concatenate([parts[3][:half].astype(bf16), narrow_sum(parts[3][half:], tail)])
    from_before = hop(forth, axis, 1)
    from_after = hop(back, axis, -1)
    return parts[0].astype(f32) + from_before.astype(f32) + from_after.astype(f32)


def turned(values, place):
    return [
        lax.dynamic_index_in_dim(values, (place + j) % 4, 0, keepdims=False) for j in range(4)
    ]


def weight_scatter(values, spot):
    y, z, c = spot
    columns = values.shape[1]
    half = columns // 2
    parts = values.reshape(4, 4, 2, 64, columns)
    mine = lax.dynamic_index_in_dim(parts, c, 2, keepdims=False)
    theirs = lax.dynamic_index_in_dim(parts, 1 - c, 2, keepdims=False)
    chip = narrow_sum(mine, hop(theirs, "core", 1))
    first = jnp.swapaxes(chip[..., :half], 0, 1).reshape(4, 256, half)
    second = chip[..., half:].reshape(4, 256, columns - half)
    first = ring_scatter(turned(first, z), "z").astype(bf16).reshape(4, 64, half)
    second = ring_scatter(turned(second, y), "y").astype(bf16).reshape(4, 64, columns - half)
    first = ring_scatter(turned(first, y), "y")
    second = ring_scatter(turned(second, z), "z")
    return jnp.concatenate([first, second], axis=1)


def small_gather(values):
    values = jnp.stack([values, hop(values, "core", 1)])
    for axis in ("z", "y"):
        values = jnp.stack([values] + [hop(values, axis, -d) for d in range(1, 4)])
    return values


def small_scatter(values, spot):
    y, z, c = spot
    parts = values.reshape((4, 4, 2) + values.shape[1:])
    mine = lax.dynamic_index_in_dim(parts, c, 2, keepdims=False)
    theirs = lax.dynamic_index_in_dim(parts, 1 - c, 2, keepdims=False)
    chip = mine + hop(theirs, "core", 1)
    for axis, place in (("y", y), ("z", z)):
        pieces = turned(chip, place)
        chip = pieces[0]
        for d in range(1, 4):
            chip = chip + hop(pieces[d], axis, d)
    return chip


def product(operand, weight, out=f32):
    return jnp.dot(operand, weight, preferred_element_type=f32).astype(out)


def product_back(operand, weight, out=f32):
    return lax.dot_general(
        operand, weight, (((1,), (1,)), ((), ())), preferred_element_type=f32
    ).astype(out)


def product_outer(operand, weight, out=bf16):
    return lax.dot_general(
        operand, weight, (((0,), (0,)), ((), ())), preferred_element_type=f32
    ).astype(out)


def norm_factor(values):
    return lax.rsqrt(jnp.mean(values * values, axis=1, keepdims=True) + eps_norm)


def normalize_back(gradient, values, factor, gains):
    weighted = gradient * gains
    return factor * weighted - values * (factor * factor * factor) * jnp.mean(
        weighted * values, axis=1, keepdims=True
    )


def sigmoid(values):
    return 1.0 / (1.0 + jnp.exp(-values))


def one_minus_exp(values):
    series = 1.0 + values * (1.0 / 8.0)
    for order in (7.0, 6.0, 5.0, 4.0, 3.0, 2.0):
        series = 1.0 + values * series * (1.0 / order)
    return jnp.where(values > -0.35, -values * series, 1.0 - jnp.exp(values))


def gelu_parts(values):
    root = 0.7978845608028654
    square = values * values
    bent = jnp.tanh(root * values * (1.0 + 0.044715 * square))
    half = 0.5 * (1.0 + bent)
    slope = half + 0.5 * values * (1.0 - bent * bent) * root * (1.0 + 3.0 * 0.044715 * square)
    return values * half, slope


def rows_at(start, size):
    return pl.ds(pl.multiple_of(start, size), size)


def conv_rows(ci_ref, slot, tile):
    base = slot * OWN + tile * HALO
    before = jnp.where(tile == 0, MEMBERS * OWN + slot * HALO, base - HALO)
    return jnp.concatenate(
        [ci_ref[rows_at(before, HALO), :].astype(f32), ci_ref[rows_at(base, HALO), :].astype(f32)],
        axis=0,
    )


def local_forward_kernel(
    ci_ref,
    place_ref,
    taps_ref,
    shift_ref,
    gates_ref,
    bias_ref,
    soft_ref,
    conv_ref,
    rate_ref,
    entry_ref,
    local_ref,
    cum_ref,
    edge_ref,
    pre_ref,
    high_ref,
    low_ref,
):
    channels = conv_ref.shape[1]

    for slot in range(MEMBERS):

        def convolve(tile, carry):
            base = slot * OWN + tile * HALO
            rows = conv_rows(ci_ref, slot, tile)
            places = place_ref[rows_at(base, HALO), :]
            total = shift_ref[...] + taps_ref[0:1, :] * rows[HALO:]
            for tap in range(1, CONV):
                lagged = pltpu.roll(rows, tap, 0)[HALO:]
                total = total + taps_ref[tap : tap + 1, :] * jnp.where(places >= tap, lagged, 0.0)
            conv_ref[rows_at(base, HALO), :] = total
            high = total.astype(bf16)
            high_ref[rows_at(base, HALO), :] = high
            low_ref[rows_at(base, HALO), :] = (total - high.astype(f32)).astype(bf16)
            return carry

        lax.fori_loop(0, OWN // HALO, convolve, 0)

    def gate(step, carry):
        columns = pl.ds(pl.multiple_of(step * 256, 256), 256)
        weight = gates_ref[:, columns]
        pre_ref[:, columns] = (
            jnp.dot(high_ref[...], weight, preferred_element_type=f32)
            + jnp.dot(low_ref[...], weight, preferred_element_type=f32)
            + bias_ref[:, columns]
        )
        return carry

    lax.fori_loop(0, 2 * channels // 256, gate, 0)

    row_ids = lax.broadcasted_iota(jnp.int32, (8, channels), 0)

    def scan(tile, carry):
        ends = []
        for slot in range(MEMBERS):
            base = slot * OWN + tile * 8
            rows = rows_at(base, 8)
            rates = sigmoid(pre_ref[rows, :channels])
            entries = sigmoid(pre_ref[rows, channels:])
            log_keep = -soft_ref[...] * rates
            resets = place_ref[rows, :] == 0
            keeps = jnp.where(resets, 0.0, jnp.exp(log_keep))
            scaling = jnp.where(resets, 1.0, jnp.sqrt(one_minus_exp(2.0 * log_keep)))
            value = entries * conv_ref[rows, :] * scaling
            coeff = keeps
            for distance in (1, 2, 4):
                reach = row_ids >= distance
                value = value + coeff * jnp.where(reach, pltpu.roll(value, distance, 0), 0.0)
                coeff = coeff * jnp.where(reach, pltpu.roll(coeff, distance, 0), 1.0)
            cum, state = carry[2 * slot], carry[2 * slot + 1]
            value = value + coeff * state
            coeff = coeff * cum
            rate_ref[rows, :] = rates
            entry_ref[rows, :] = entries
            local_ref[rows, :] = value
            cum_ref[rows, :] = coeff
            ends += [coeff[7:8], value[7:8]]
        return tuple(ends)

    start = (jnp.ones((1, channels), f32), jnp.zeros((1, channels), f32)) * MEMBERS
    ends = lax.fori_loop(0, OWN // 8, scan, start)
    edge_ref[...] = jnp.concatenate(ends[0::2] + ends[1::2], axis=0)


def place_of(spot_ref, tok):
    y, z, c = spot_ref[0], spot_ref[1], spot_ref[2]
    far_y = jnp.bitwise_and((tok >> 3) - y + 4, 3)
    far_z = jnp.bitwise_and(jnp.bitwise_and(tok >> 1, 3) - z + 4, 3)
    far_c = jnp.bitwise_xor(jnp.bitwise_and(tok, 1), c)
    return far_y * 8 + far_z * 2 + far_c


def mix_kernel(spot_ref, edges_ref, local_ref, cum_ref, branch_ref, state_ref, mixed_ref, carry_ref):
    channels = local_ref.shape[1]
    tok = spot_ref[3]

    def fold(at, pair):
        block = edges_ref[place_of(spot_ref, at)]
        return pair[0] * block[:4], block[:4] * pair[1] + block[4:]

    whole = (jnp.ones((4, channels), f32), jnp.zeros((4, channels), f32))
    prefix = lax.fori_loop(0, tok, fold, whole)
    total = lax.fori_loop(tok, TOKS, fold, prefix)
    current = jnp.zeros((1, channels), f32)
    carries = [None] * MEMBERS
    for _ in range(2):
        for slot in range(MEMBERS):
            one = slice(slot, slot + 1)
            carries[slot] = prefix[0][one] * current + prefix[1][one]
            current = total[0][one] * current + total[1][one]
    carry_ref[...] = jnp.concatenate(carries, axis=0)

    def apply(tile, token):
        for slot in range(MEMBERS):
            rows = rows_at(slot * OWN + tile * HALO, HALO)
            states = local_ref[rows, :] + cum_ref[rows, :] * carry_ref[slot : slot + 1, :]
            state_ref[rows, :] = states
            mixed_ref[rows, :] = (states * gelu_parts(branch_ref[rows, :])[0]).astype(bf16)
        return token

    lax.fori_loop(0, OWN // HALO, apply, 0)


def local_backward_kernel(
    grad_ref,
    branch_ref,
    state_ref,
    rate_ref,
    place_ref,
    soft_ref,
    bgrad_ref,
    sgrad_ref,
    local_ref,
    cum_ref,
    edge_ref,
):
    channels = grad_ref.shape[1]
    row_ids = lax.broadcasted_iota(jnp.int32, (8, channels), 0)

    def scan(step, carry):
        ends = []
        for slot in range(MEMBERS):
            pieces = {}
            base = slot * OWN + OWN - HALO - step * HALO
            cum, after = carry[2 * slot], carry[2 * slot + 1]
            slopes = []
            for part in (1, 0):
                rows = rows_at(base + 8 * part, 8)
                gated, slope = gelu_parts(branch_ref[rows, :])
                gradient = grad_ref[rows, :]
                slopes.append(slope * gradient * state_ref[rows, :])
                sgrad = gradient * gated
                keeps = jnp.where(
                    place_ref[rows, :] == 0, 0.0, jnp.exp(-soft_ref[...] * rate_ref[rows, :])
                )
                coeff = keeps
                value = keeps * sgrad
                for distance in (1, 2, 4):
                    reach = row_ids < 8 - distance
                    value = value + coeff * jnp.where(
                        reach, pltpu.roll(value, 8 - distance, 0), 0.0
                    )
                    coeff = coeff * jnp.where(reach, pltpu.roll(coeff, 8 - distance, 0), 1.0)
                value = value + coeff * after
                coeff = coeff * cum
                sgrad_ref[rows, :] = sgrad
                local_ref[rows, :] = value
                cum_ref[rows, :] = coeff
                cum, after = coeff[0:1], value[0:1]
            bgrad_ref[rows_at(base, HALO), :] = jnp.concatenate(
                [slopes[1], slopes[0]], axis=0
            ).astype(bf16)
            ends += [cum, after]
        return tuple(ends)

    start = (jnp.ones((1, channels), f32), jnp.zeros((1, channels), f32)) * MEMBERS
    ends = lax.fori_loop(0, OWN // HALO, scan, start)
    edge_ref[...] = jnp.concatenate(ends[0::2] + ends[1::2], axis=0)


def finish_backward_kernel(
    spot_ref,
    edges_ref,
    sgrad_ref,
    local_ref,
    cum_ref,
    state_ref,
    carry_ref,
    conv_ref,
    rate_ref,
    entry_ref,
    place_ref,
    soft_ref,
    ci_ref,
    taps_ref,
    gates_ref,
    pregrad_ref,
    igrad_ref,
    owed_ref,
    sums_ref,
    tapsum_ref,
    cgrad_ref,
    back_ref,
):
    channels = conv_ref.shape[1]
    tok = spot_ref[3]

    def fold(step, pair):
        block = edges_ref[place_of(spot_ref, TOKS - 1 - step)]
        return pair[0] * block[:4], block[:4] * pair[1] + block[4:]

    whole = (jnp.ones((4, channels), f32), jnp.zeros((4, channels), f32))
    prefix = lax.fori_loop(0, TOKS - 1 - tok, fold, whole)
    total = lax.fori_loop(TOKS - 1 - tok, TOKS, fold, prefix)
    current = jnp.zeros((1, channels), f32)
    carries = [None] * MEMBERS
    for _ in range(2):
        for slot in reversed(range(MEMBERS)):
            one = slice(slot, slot + 1)
            carries[slot] = prefix[0][one] * current + prefix[1][one]
            current = total[0][one] * current + total[1][one]
    back_ref[...] = jnp.concatenate(carries, axis=0)

    row_ids = lax.broadcasted_iota(jnp.int32, (8, channels), 0)
    zero = jnp.zeros((8, channels), f32)
    logit_sum, rate_sum, entry_sum = zero, zero, zero
    for slot in range(MEMBERS):

        def gate_grads(step, carry):
            later, logit_sum, rate_sum, entry_sum = carry
            base = slot * OWN + OWN - HALO - step * HALO
            low_rate, low_entry = [], []
            for part in (1, 0):
                first = base + 8 * part
                rows = rows_at(first, 8)
                held = local_ref[rows, :] + cum_ref[rows, :] * back_ref[slot : slot + 1, :]
                following = jnp.where(row_ids == 7, later, pltpu.roll(held, 7, 0))
                adjoint = sgrad_ref[rows, :] + following
                later = held[0:1]
                ahead = state_ref[rows_at(jnp.maximum(first - 8, 0), 8), :][7:8]
                at_start = first == slot * OWN
                ahead = jnp.where(at_start, carry_ref[slot : slot + 1, :], ahead)
                previous = jnp.where(row_ids == 0, ahead, pltpu.roll(state_ref[rows, :], 1, 0))
                rates, entries, conv = rate_ref[rows, :], entry_ref[rows, :], conv_ref[rows, :]
                resets = place_ref[rows, :] == 0
                log_keep = -soft_ref[...] * rates
                squared = jnp.exp(2.0 * log_keep)
                root = jnp.sqrt(one_minus_exp(2.0 * log_keep))
                scaling = jnp.where(resets, 1.0, root)
                turn = jnp.where(resets, 0.0, squared / root)
                weighed = adjoint * entries
                log_grad = held * previous - weighed * conv * turn
                rate_part = log_grad * rates
                logit_sum = logit_sum + rate_part
                rate_grad = -soft_ref[...] * rate_part * (1.0 - rates)
                direct = weighed * scaling
                entry_grad = direct * conv * (1.0 - entries)
                rate_sum = rate_sum + rate_grad
                entry_sum = entry_sum + entry_grad
                cgrad_ref[rows, :] = direct
                low_rate.append(rate_grad)
                low_entry.append(entry_grad)
            rows = rows_at(base, HALO)
            pregrad_ref[rows, :channels] = jnp.concatenate(low_rate[::-1], axis=0).astype(bf16)
            pregrad_ref[rows, channels:] = jnp.concatenate(low_entry[::-1], axis=0).astype(bf16)
            return later, logit_sum, rate_sum, entry_sum

        _, logit_sum, rate_sum, entry_sum = lax.fori_loop(
            0,
            OWN // HALO,
            gate_grads,
            (back_ref[slot : slot + 1, :], logit_sum, rate_sum, entry_sum),
        )

    def gate_back(step, carry):
        columns = pl.ds(pl.multiple_of(step * 128, 128), 128)
        cgrad_ref[:, columns] += jnp.dot(
            pregrad_ref[...], gates_ref[:, columns], preferred_element_type=f32
        )
        return carry

    lax.fori_loop(0, channels // 128, gate_back, 0)

    shift_sum = jnp.zeros((HALO, channels), f32)
    tap_sums = [shift_sum] * CONV
    for slot in range(MEMBERS):

        def spread(rows, places):
            return [rows] + [jnp.where(places >= tap, rows, 0.0) for tap in range(1, CONV)]

        def shifted_sum(current, following):
            total = taps_ref[0:1, :] * current[0]
            for tap in range(1, CONV):
                both = jnp.concatenate([current[tap], following[tap]], axis=0)
                total = total + taps_ref[tap : tap + 1, :] * pltpu.roll(both, 2 * HALO - tap, 0)[:HALO]
            return total

        def conv_back(tile, carry):
            shift_sum, tap_sums = carry
            base = slot * OWN + tile * HALO
            rows = rows_at(base, HALO)
            after = jnp.minimum(base + HALO, slot * OWN + OWN - HALO)
            next_rows = rows_at(after, HALO)
            last = jnp.where(tile == OWN // HALO - 1, 0.0, 1.0)
            grads = spread(cgrad_ref[rows, :], place_ref[rows, :])
            coming = spread(cgrad_ref[next_rows, :] * last, place_ref[next_rows, :])
            igrad_ref[rows, :] = shifted_sum(grads, coming)
            inputs = conv_rows(ci_ref, slot, tile)
            shift_sum = shift_sum + grads[0]
            sums = [tap_sums[0] + grads[0] * inputs[HALO:]]
            for tap in range(1, CONV):
                sums.append(tap_sums[tap] + grads[tap] * pltpu.roll(inputs, tap, 0)[HALO:])
            return shift_sum, sums

        shift_sum, tap_sums = lax.fori_loop(0, OWN // HALO, conv_back, (shift_sum, tap_sums))
        rows = rows_at(slot * OWN, HALO)
        first = spread(cgrad_ref[rows, :], place_ref[rows, :])
        owed_ref[slot * HALO : (slot + 1) * HALO, :] = shifted_sum(
            [jnp.zeros((HALO, channels), f32)] * CONV, first
        )

    def total_rows(values):
        return jnp.sum(values, axis=0, keepdims=True)

    sums_ref[...] = jnp.concatenate(
        [total_rows(v) for v in (shift_sum, rate_sum, entry_sum, logit_sum)], axis=0
    )
    tapsum_ref[...] = jnp.concatenate([total_rows(v) for v in tap_sums], axis=0)


def in_vmem(kernel, outs, scratch=(), scalars=0, count=1, flops=0, moved=0):
    vmem = pl.BlockSpec(memory_space=pltpu.VMEM)
    smem = pl.BlockSpec(memory_space=pltpu.SMEM)
    return pl.pallas_call(
        kernel,
        out_shape=[jax.ShapeDtypeStruct(shape, dtype) for shape, dtype in outs],
        in_specs=[smem] * scalars + [vmem] * count,
        out_specs=[vmem] * len(outs),
        scratch_shapes=[pltpu.VMEM(shape, dtype) for shape, dtype in scratch],
        compiler_params=pltpu.CompilerParams(vmem_limit_bytes=40 * 1024 * 1024),
        cost_estimate=pl.CostEstimate(flops=flops, bytes_accessed=moved, transcendentals=0),
    )


def per_device(
    inputs,
    mix_scale,
    branch_mat,
    input_mat,
    conv_taps,
    conv_shift,
    rate_mat,
    rate_shift,
    entry_mat,
    entry_shift,
    decay_logit,
    out_mat,
    feed_scale,
    gate_mat,
    up_mat,
    down_mat,
    lengths,
    cotangent,
):
    blk = lax.axis_index("blk")
    tok = lax.axis_index("tok")
    spot = (tok // 8, (tok // 2) % 4, tok % 2)
    spots = jnp.stack(list(spot) + [tok]).astype(jnp.int32)
    width = inputs.shape[1]
    channels = branch_mat.shape[1]
    hidden_units = gate_mat.shape[1]
    groups, _, block = rate_mat.shape
    slice_rows = branch_mat.shape[0]
    total_rows = MEMBERS * OWN

    smalls = [rate_mat, entry_mat, mix_scale, feed_scale, conv_taps, conv_shift]
    smalls += [rate_shift, entry_shift, decay_logit]
    flat = jnp.concatenate([member.reshape(-1) for member in smalls])
    flat = jnp.pad(flat, (0, slice_rows * 128 - flat.shape[0])).reshape(slice_rows, 128)
    mixer_all = lax.all_gather(
        jnp.concatenate([input_mat, branch_mat, out_mat.T, flat], axis=1), "tok", axis=0, tiled=True
    )
    feed_all = lax.all_gather(
        jnp.concatenate([gate_mat, up_mat, down_mat.T], axis=1), "tok", axis=0, tiled=True
    )
    input_all = mixer_all[:, :channels]
    branch_all = mixer_all[:, channels : 2 * channels]
    project_all = mixer_all[:, : 2 * channels]
    out_turned = mixer_all[:, 2 * channels : 3 * channels]
    gate_up_all = feed_all[:, : 2 * hidden_units]
    down_turned = feed_all[:, 2 * hidden_units :]
    small_all = mixer_all[:, 3 * channels :].reshape(TOKS, -1)
    cuts, at = [], 0
    for member in smalls:
        cuts.append(small_all[:, at : at + member.size].reshape((TOKS,) + member.shape))
        at += member.size
    rate_all = jnp.moveaxis(cuts[0], 0, 1).reshape(groups, block, block)
    entry_all = jnp.moveaxis(cuts[1], 0, 1).reshape(groups, block, block)
    mix_gain = cuts[2].reshape(1, -1).astype(f32)
    feed_gain = cuts[3].reshape(1, -1).astype(f32)
    taps = jnp.moveaxis(cuts[4], 0, 1).reshape(CONV, channels).astype(f32)
    shift, rate_bias, entry_bias, logits = [
        member.reshape(1, channels).astype(f32) for member in cuts[5:]
    ]
    bias = jnp.concatenate([rate_bias, entry_bias], axis=1)
    soft = decay_power * jax.nn.softplus(-logits)
    same = jnp.eye(groups, dtype=bf16)[:, None, :, None]

    def dense(mats):
        return (mats[:, :, None, :] * same).reshape(channels, channels)

    gates = jnp.concatenate([dense(rate_all), dense(entry_all)], axis=1)

    slots = (blk + jnp.arange(MEMBERS, dtype=jnp.int32)) % MEMBERS
    token_ids = (
        (slots * TOKS + tok)[:, None] * OWN + jnp.arange(OWN, dtype=jnp.int32)[None, :]
    ).reshape(-1)
    starts = jnp.cumsum(lengths) - lengths
    opened = jnp.max(jnp.where(starts[None, :] <= token_ids[:, None], starts[None, :], 0), axis=1)
    places = (token_ids - opened).reshape(total_rows, 1).astype(jnp.int32)

    devices = MEMBERS * TOKS
    tail = lax.ppermute(
        inputs[OWN - HALO :], ("blk", "tok"), [(i, (i + 1) % devices) for i in range(devices)]
    )
    rows_all = jnp.concatenate(ring_gather(inputs) + ring_gather(tail), axis=0)
    cotangent_all = jnp.concatenate(ring_gather(cotangent), axis=0)

    wide_values = rows_all.astype(f32)
    wide_one = (wide_values * norm_factor(wide_values) * mix_gain).astype(bf16)
    own_one = wide_one[:total_rows]
    conv_input = product(wide_one, input_all, bf16)
    branch = product(own_one, branch_all)
    state_shape = ((total_rows, channels), f32)
    conv, rates, entries, local, cum, edges = in_vmem(
        local_forward_kernel,
        [state_shape] * 5 + [((8, channels), f32)],
        [
            ((total_rows, 2 * channels), f32),
            ((total_rows, channels), bf16),
            ((total_rows, channels), bf16),
        ],
        count=7,
    )(conv_input, places, taps, shift, gates, bias, soft)
    all_edges = small_gather(edges).reshape(TOKS, 8, channels)
    states, mixture, carried = in_vmem(
        mix_kernel,
        [state_shape, ((total_rows, channels), bf16), ((MEMBERS, channels), f32)],
        scalars=1,
        count=4,
    )(spots, all_edges, local, cum, branch)

    def rows_of(values):
        return [values[j * OWN : (j + 1) * OWN] for j in range(MEMBERS)]

    own_values = inputs.astype(f32)
    middle = own_values + ring_scatter(rows_of(product_back(mixture, out_turned)))

    factor_two = norm_factor(middle)
    normed_two = (middle * factor_two * feed_gain).astype(bf16)
    wide_two = jnp.concatenate(ring_gather(normed_two), axis=0)
    gate_up = product(wide_two, gate_up_all)
    gate_pre, up_pre = gate_up[:, :hidden_units], gate_up[:, hidden_units:]
    hidden_grad = product(cotangent_all, down_turned)
    gate_act, gate_slope = gelu_parts(gate_pre)
    hidden = (gate_act * up_pre).astype(bf16)
    gate_grad = (gate_slope * hidden_grad * up_pre).astype(bf16)
    up_grad = (gate_act * hidden_grad).astype(bf16)
    both_grads = jnp.concatenate([gate_grad, up_grad], axis=1)
    two_shares = product_back(both_grads, gate_up_all)
    two_grad = ring_scatter(rows_of(two_shares))
    middle_grad = cotangent.astype(f32) + normalize_back(two_grad, middle, factor_two, feed_gain)
    layer_out = middle + ring_scatter(rows_of(product_back(hidden, down_turned)))
    grad_feed_scale = jnp.sum(two_grad * middle * factor_two, axis=0)
    grad_gate_up = lax.psum_scatter(
        product_outer(wide_two, both_grads), "tok", scatter_dimension=0, tiled=True
    )
    grad_down = lax.psum_scatter(
        product_outer(cotangent_all, hidden), "tok", scatter_dimension=0, tiled=True
    )

    middle_wide = jnp.concatenate(ring_gather(middle_grad.astype(bf16)), axis=0)
    mixture_grad = product(middle_wide, out_turned)
    branch_grad, sgrad, local_back, cum_back, back_edges = in_vmem(
        local_backward_kernel,
        [((total_rows, channels), bf16)] + [state_shape] * 3 + [((8, channels), f32)],
        count=6,
    )(mixture_grad, branch, states, rates, places, soft)
    all_back = small_gather(back_edges).reshape(TOKS, 8, channels)
    pregrads, igrad, owed, sums, tap_sums = in_vmem(
        finish_backward_kernel,
        [
            ((total_rows, 2 * channels), bf16),
            state_shape,
            ((MEMBERS * HALO, channels), f32),
            ((4, channels), f32),
            ((CONV, channels), f32),
        ],
        [((total_rows, channels), f32), ((MEMBERS, channels), f32)],
        scalars=1,
        count=14,
    )(
        spots,
        all_back,
        sgrad,
        local_back,
        cum_back,
        states,
        carried,
        conv,
        rates,
        entries,
        places,
        soft,
        conv_input,
        taps,
        gates.T,
    )
    returned = lax.ppermute(
        owed.reshape(MEMBERS, HALO, channels)[:, HALO - 3 :],
        "tok",
        [(i, (i - 1) % TOKS) for i in range(TOKS)],
    )
    turned_on = jnp.concatenate([returned[1:], returned[:1]], axis=0)
    landing = jnp.where(tok == TOKS - 1, turned_on, returned)
    input_grad = igrad.reshape(MEMBERS, OWN, channels) + jnp.pad(
        landing, ((0, 0), (OWN - 3, 0), (0, 0))
    )
    input_low = input_grad.reshape(total_rows, channels).astype(bf16)
    one_shares = product_back(input_low, input_all) + product_back(branch_grad, branch_all)
    one_grad = ring_scatter(rows_of(one_shares))
    factor_one = norm_factor(own_values)
    first_grad = normalize_back(one_grad, own_values, factor_one, mix_gain)
    inputs_grad = (middle_grad + first_grad).astype(bf16)
    grad_mix_scale = jnp.sum(one_grad * own_values * factor_one, axis=0)

    grad_early = weight_scatter(
        jnp.concatenate(
            [product_outer(own_one, branch_grad), product_outer(middle_wide, mixture)], axis=1
        ),
        spot,
    )
    grad_branch, grad_out = grad_early[:, :channels], grad_early[:, channels:]
    grad_input = weight_scatter(product_outer(own_one, input_low), spot)
    dense_grads = product_outer(conv.astype(bf16), pregrads, f32)
    columns = jnp.arange(2 * channels, dtype=jnp.int32) % channels // block
    gate_grads = sum(
        jnp.where(columns == h, dense_grads[h * block : (h + 1) * block], 0.0)
        for h in range(groups)
    )
    small_grads = [
        gate_grads.reshape(TOKS, -1),
        jnp.moveaxis(tap_sums.reshape(CONV, TOKS, -1), 1, 0).reshape(TOKS, -1),
        jnp.moveaxis(sums.reshape(4, TOKS, -1), 1, 0).reshape(TOKS, -1),
        grad_mix_scale.reshape(TOKS, -1),
        grad_feed_scale.reshape(TOKS, -1),
    ]
    settled = small_scatter(jnp.concatenate(small_grads, axis=1), spot)
    cuts, at = [], 0
    for member in small_grads:
        cuts.append(settled[at : at + member.shape[1]])
        at += member.shape[1]
    gate_own = jnp.transpose(cuts[0].reshape(block // TOKS, 2, groups, block), (1, 2, 0, 3))
    sums_own = cuts[2].reshape(4, -1)
    gains_own = jnp.concatenate(cuts[3:])
    gains_own = gains_own + hop_blk(gains_own, 1) + hop_blk(gains_own, -1) + hop_blk(gains_own, 2)
    own_logits = decay_logit.astype(f32)
    return (
        layer_out.astype(bf16),
        inputs_grad,
        gains_own[: width // TOKS],
        grad_branch,
        grad_input,
        cuts[1].reshape(CONV, -1),
        sums_own[0],
        gate_own[0],
        sums_own[1],
        gate_own[1],
        sums_own[2],
        sums_own[3] * decay_power * jax.nn.sigmoid(-own_logits),
        grad_out.T,
        gains_own[width // TOKS :],
        grad_gate_up[:, :hidden_units].astype(f32),
        grad_gate_up[:, hidden_units:].astype(f32),
        grad_down.T.astype(f32),
    )


def solution(mesh):
    in_specs = (
        P(("blk", "tok"), None),
        P("tok"),
        P("tok", "blk"),
        P("tok", "blk"),
        P(None, ("blk", "tok")),
        P(("blk", "tok")),
        P("blk", "tok", None),
        P(("blk", "tok")),
        P("blk", "tok", None),
        P(("blk", "tok")),
        P(("blk", "tok")),
        P("blk", "tok"),
        P("tok"),
        P("tok", "blk"),
        P("tok", "blk"),
        P("blk", "tok"),
        P(),
        P(("blk", "tok"), None),
    )
    out_specs = (
        P(("blk", "tok"), None),
        P(("blk", "tok"), None),
        P("tok"),
        P("tok", "blk"),
        P("tok", "blk"),
        P(None, ("blk", "tok")),
        P(("blk", "tok")),
        P("blk", "tok", None),
        P(("blk", "tok")),
        P("blk", "tok", None),
        P(("blk", "tok")),
        P(("blk", "tok")),
        P("blk", "tok"),
        P("tok"),
        P("tok", "blk"),
        P("tok", "blk"),
        P("blk", "tok"),
    )
    return jax.shard_map(
        per_device, mesh=mesh, in_specs=in_specs, out_specs=out_specs, check_vma=False
    )
```

time: 1740 us -> 538 us (0.31)
  the two profiles are of different devices: /device:TPU:0 before, /device:TPU:4 now
where the time goes in v1:
time: 538 us; the launch traced here: 533 us
  waiting for transfers between devices  157 us (29%)
  starting transfers between devices  125 us (23%)
  matrix products  90.1 us (17%)
  local copies, waits for them, and re-layouts  75.8 us (14%)
  other arithmetic  43.5 us (8%)
  Pallas kernels  26.3 us (5%)
  between operations  15.7 us (3%)
    ppermute x39, waiting for transfers between devices, hop_blk(): lax.ppermute(values, 'blk', [(i, (i + distance) % MEMBERS) for i in range...  79.9 us
    ppermute x55, starting transfers between devices, hop_tok(): return lax.ppermute(values, 'tok', route)  74.2 us
    ppermute x39, starting transfers between devices, hop_blk(): lax.ppermute(values, 'blk', [(i, (i + distance) % MEMBERS) for i in range...  47.8 us
    ppermute x55, waiting for transfers between devices, hop_tok(): return lax.ppermute(values, 'tok', route)  46.9 us
    dot_general x5, matrix products, product(): return jnp.dot(operand, weight, preferred_element_type=f32).astype(out)  32.4 us
    dot_general x5, matrix products, product_back(): lax.dot_general(operand, weight, (((1,), (1,)), ((), ())), preferred_elem...  30.9 us
    unnamed x139, local copies, waits for them, and re-layouts  27.2 us
    dot_general x6, matrix products, product_outer(): lax.dot_general(operand, weight, (((0,), (0,)), ((), ())), preferred_elem...  26.9 us
  transfers between devices with their start and end apart: 100, of which 43 were waited for; matrix products, arithmetic and copies ran while one was open for 30% of the time, Pallas kernels for 5%

profile of v1, /device:TPU:4, one launch (start us, length us, event | category | flops | bytes accessed | tf_op | source)
XLA Modules:
  0.0 533.2 jit_solution(15752021173994744909)
XLA Ops:
  9.7 4.1 concatenate.131
  20.1 17.5 %collective-permute-done.4 = bf16[16,2048]{1,0:T(8,128)(2,1)} collective-permute-done((bf16[16,2048]{1,0:T(8,128)(2,1)S(1)}, bf16[16,2048]{1,0:T(8,128)(2,1)}, u32[]{:S(2)}, u32[]{:S(2)}) %collective-permute-start.4) | collective-permute-done | bytes 65568 | tf_op jit(solution)/shard_map/ppermute | solution.py:597
  44.5 3.0 collective-permute-start.7
  51.1 4.3 collective-permute-done.3
  58.1 12.9 %all-gather.3.cloned.1.call-done = bf16[2048,2048]{1,0:T(8,128)(2,1)} async-done(((bf16[64,2048]{1,0:T(8,128)(2,1)}), bf16[2048,2048]{1,0:T(8,128)(2,1)}) %all-gather.3.cloned.1.call-update) | async-done | bytes 8388624 | tf_op jit(solution)/shard_map/all_gather | solution.py:554
  87.3 2.7 copy.83.gates_ref
  93.9 3.8 fusion.28.ci_ref
  97.7 9.8 %shard_map.305 = (f32[512,640]{1,0:T(8,128)S(1)}, f32[512,640]{1,0:T(8,128)S(1)}, f32[512,640]{1,0:T(8,128)S(1)}, f32[512,640]{1,0:T(8,128)S(1)}, f32[512,640]{1,0:T(8,128)S(1)}, /*index=5*/f32[8,640]{1,0:T(8,128)S(1)}) custom-call(bf16[576,640]{1,0:T(8,128)(2,1)S(1)} %fusion.28.ci_ref, s32[512,1]{1,0:T(8,128)S(1)} %sub.49.place_ref, ...), custom_call_target="tpu_custom_call" | custom-call | tf_op jit(solution)/shard_map/pallas_call | solution.py:609
  113.0 2.8 collective-permute-start.11
  127.2 4.4 fusion.19.branch_ref
  131.6 3.5 collective-permute-done.14
  135.1 5.4 %collective-permute-done.13 = f32[4,2,8,640]{3,2,1,0:T(8,128)S(1)} collective-permute-done((f32[4,2,8,640]{3,2,1,0:T(8,128)S(1)}, f32[4,2,8,640]{3,2,1,0:T(8,128)S(1)}, u32[]{:S(2)}, u32[]{:S(2)}) %collective-permute-start.13) | collective-permute-done | bytes 163872 | tf_op jit(solution)/shard_map/ppermute | solution.py:38
  142.3 4.3 fusion.114
  150.8 5.2 collective-permute-done.16
  160.5 8.0 %collective-permute-done.28 = bf16[128,2048]{1,0:T(8,128)(2,1)S(1)} collective-permute-done((bf16[128,2048]{1,0:T(8,128)(2,1)S(1)}, bf16[128,2048]{1,0:T(8,128)(2,1)S(1)}, u32[]{:S(2)}, u32[]{:S(2)}) %collective-permute-start.28) | collective-permute-done | bytes 524320 | tf_op jit(solution)/shard_map/ppermute | solution.py:21
  172.8 6.5 %collective-permute-done.19 = bf16[128,2048]{1,0:T(8,128)(2,1)} collective-permute-done((bf16[128,2048]{1,0:T(8,128)(2,1)S(1)}, bf16[128,2048]{1,0:T(8,128)(2,1)}, u32[]{:S(2)}, u32[]{:S(2)}) %collective-permute-start.19) | collective-permute-done | bytes 524320 | tf_op jit(solution)/shard_map/ppermute | solution.py:21
  186.6 7.9 %collective-permute-done.21 = bf16[128,2048]{1,0:T(8,128)(2,1)S(1)} collective-permute-done((bf16[128,2048]{1,0:T(8,128)(2,1)S(1)}, bf16[128,2048]{1,0:T(8,128)(2,1)S(1)}, u32[]{:S(2)}, u32[]{:S(2)}) %collective-permute-start.21) | collective-permute-done | bytes 524320 | tf_op jit(solution)/shard_map/ppermute | solution.py:21
  197.8 3.1 collective-permute-done.22
  204.6 12.1 %fusion.2 = f32[512,3072]{1,0:T(8,128)} fusion(bf16[512,2048]{1,0:T(8,128)(2,1)} %constant_dynamic-update-slice_fusion.12, bf16[2048,4608]{1,0:T(8,128)(2,1)} %all-gather.5.cloned.1.call-done), kind=kOutput, calls=%fused_computation.3 | convolution fusion | flops 6442450944 | bytes 20971520 | tf_op jit(solution)/shard_map/dot_general | solution.py:116
  218.1 8.4 %multiply_convert_fusion.1 = (bf16[512,1536]{1,0:T(8,128)(2,1)}, bf16[512,1536]{1,0:T(8,128)(2,1)}, bf16[512,1536]{1,0:T(8,128)(2,1)S(1)}) fusion(f32[512,3072]{1,0:T(8,128)} %fusion.2, bf16[512,2048]{1,0:T(8,128)(2,1)S(1)} %copy-done.50, bf16[2048,4608]{1,0:T(8,128)(2,1)S(1)} %copy-done.55), kind=kOutput, calls=%fused_computation.23 | convolution fusion | flops 3240099840 | bytes 19398656 | tf_op jit(solution)/shard_map/dot_general | solution.py:116
  227.7 5.4 %convolution_convert_fusion.1 = bf16[2048,1536]{1,0:T(8,128)(2,1)} fusion(bf16[512,2048]{1,0:T(8,128)(2,1)S(1)} %copy-done.50, bf16[512,1536]{1,0:T(8,128)(2,1)S(1)} %get-tuple-element.72), kind=kOutput, calls=%fused_computation.5 | convolution fusion | flops 3224371200 | bytes 9961472 | tf_op jit(solution)/shard_map/dot_general | solution.py:126
  233.2 6.0 %fusion.116 = (bf16[512,2048]{1,0:T(8,128)(2,1)S(1)}, f32[512,2048]{1,0:T(8,128)S(1)}) fusion(bf16[512,1536]{1,0:T(8,128)(2,1)} %copy-done.57, bf16[2048,4608]{1,0:T(8,128)(2,1)} %all-gather.5.cloned.1.call-done), kind=kOutput, calls=%fused_computation.350 | convolution fusion | flops 3222274048 | bytes 14155776 | tf_op jit(solution)/shard_map/dot_general | solution.py:120
  241.5 11.0 %fusion.115 = (bf16[512,2048]{1,0:T(8,128)(2,1)S(1)}, f32[512,2048]{1,0:T(8,128)S(1)}) fusion(bf16[2048,4608]{1,0:T(8,128)(2,1)} %all-gather.5.cloned.1.call-done, bf16[512,1536]{1,0:T(8,128)(2,1)} %get-tuple-element.71, bf16[512,1536]{1,0:T(8,128)(2,1)} %get-tuple-element.70), kind=kOutput, calls=%fused_computation.349 | convolution fusion | flops 6449790976 | bytes 22020096 | tf_op jit(solution)/shard_map/dot_general | solution.py:120
  257.4 4.4 collective-permute-done.32
  266.5 5.3 collective-permute-done.27
  271.8 5.6 %collective-permute-done.35 = bf16[128,2048]{1,0:T(8,128)(2,1)S(1)} collective-permute-done((bf16[128,2048]{1,0:T(8,128)(2,1)S(1)}, bf16[128,2048]{1,0:T(8,128)(2,1)S(1)}, u32[]{:S(2)}, u32[]{:S(2)}) %collective-permute-start.35) | collective-permute-done | bytes 524320 | tf_op jit(solution)/shard_map/ppermute | solution.py:21
  280.5 2.9 collective-permute-start.37
  283.6 9.7 %collective-permute-done.37 = bf16[128,2048]{1,0:T(8,128)(2,1)S(1)} collective-permute-done((bf16[128,2048]{1,0:T(8,128)(2,1)}, bf16[128,2048]{1,0:T(8,128)(2,1)S(1)}, u32[]{:S(2)}, u32[]{:S(2)}) %collective-permute-start.37) | collective-permute-done | bytes 524320 | tf_op jit(solution)/shard_map/ppermute | solution.py:21
  296.4 12.0 %convolution_convert_fusion = bf16[2048,3072]{1,0:T(8,128)(2,1)} fusion(bf16[512,2048]{1,0:T(8,128)(2,1)} %constant_dynamic-update-slice_fusion.12, bf16[512,1536]{1,0:T(8,128)(2,1)} %get-tuple-element.71, bf16[512,1536]{1,0:T(8,128)(2,1)} %get-tuple-element.70), kind=kOutput, calls=%fused_computation | convolution fusion | flops 6455033856 | bytes 17825792 | tf_op jit(solution)/shard_map/dot_general | solution.py:126
  311.7 3.9 collective-permute-done.39
  317.1 3.3 convolution_convert_fusion.3
  320.5 3.7 fusion.14.grad_ref
  332.1 2.8 pad_maximum_fusion
  334.8 8.2 %copy.86 = bf16[2048,1280]{1,0:T(8,128)(2,1)} copy(bf16[2048,1280]{0,1:T(8,128)(2,1)} %pad_maximum_fusion) | data formatting | bytes 10485760 | tf_op jit(solution)/shard_map/concatenate | solution.py:712
  347.3 3.9 dynamic-slice_bitcast_fusion
  355.8 12.3 %shard_map.308 = (bf16[512,1280]{1,0:T(8,128)(2,1)S(1)}, f32[512,640]{1,0:T(8,128)S(1)}, f32[64,640]{1,0:T(8,128)S(1)}, f32[4,640]{1,0:T(4,128)S(1)}, f32[4,640]{1,0:T(4,128)S(1)}) custom-call(s32[4]{0:T(128)S(1)} %pad_add_fusion.spot_ref, f32[32,8,640]{2,1,0:T(8,128)S(1)} %bitcast.293, f32[512,640]{1,0:T(8,128)S(1)} %copy-done.16, ...), custom_call_target="tpu_custom_call" | custom-call | tf_op jit(solution)/shard_map/pallas_call | solution.py:664
  370.5 2.7 fusion.52
  376.6 3.8 fusion.21
  380.4 5.8 %fusion.117 = (bf16[512,2048]{1,0:T(8,128)(2,1)S(1)}, f32[512,2048]{1,0:T(8,128)}) fusion(f32[512,2048]{1,0:T(8,128)S(1)} %fusion.21, bf16[512,640]{1,0:T(8,128)(2,1)S(1)} %copy-done.23, bf16[2048,2048]{1,0:T(8,128)(2,1)} %all-gather.3.cloned.1.call-done), kind=kOutput, calls=%fused_computation.351 | convolution fusion | flops 1344274432 | bytes 13762560 | tf_op jit(solution)/shard_map/dot_general | solution.py:120
  387.0 3.1 collective-permute-start.48
  391.3 3.3 collective-permute-done.48
  403.9 5.9 %collective-permute-done.51 = bf16[128,2048]{1,0:T(8,128)(2,1)S(1)} collective-permute-done((bf16[128,2048]{1,0:T(8,128)(2,1)S(1)}, bf16[128,2048]{1,0:T(8,128)(2,1)S(1)}, u32[]{:S(2)}, u32[]{:S(2)}) %collective-permute-start.51) | collective-permute-done | bytes 524320 | tf_op jit(solution)/shard_map/ppermute | solution.py:21
  415.0 2.7 fusion.35
  427.1 3.9 collective-permute-done.54
  431.9 2.8 collective-permute-start.58
  436.6 3.5 collective-permute-done.57
  441.0 2.7 collective-permute-start.61
  449.8 3.1 collective-permute-start.82
  453.7 2.9 collective-permute-start.75
  456.9 3.1 collective-permute-start.83
  460.1 3.5 collective-permute-done.73
  463.8 3.2 collective-permute-start.78
  467.2 3.2 collective-permute-start.86
  472.7 2.9 collective-permute-start.87
  477.6 3.4 collective-permute-done.85
  481.0 3.3 fusion.8
  484.9 3.2 collective-permute-start.90
  489.2 3.2 collective-permute-start.65
  496.6 2.6 collective-permute-start.66
  500.2 3.1 collective-permute-done.89
  503.5 3.2 collective-permute-start.94
  507.8 3.2 collective-permute-start.69
  513.3 3.0 collective-permute-start.70
  518.5 3.6 collective-permute-done.68
  (480 shorter events, 193.4 us)
Async XLA Ops:
  7.2 63.8 %all-gather.3.cloned.1.call-start = ((), (), s32[]{:S(2)}) async-start(), calls=%async_computation.2 | async-start | bytes 8650752 | tf_op jit(solution)/shard_map/all_gather | solution.py:554
  15.5 189.1 %all-gather.5.cloned.1.call-start = ((), (), s32[]{:S(2)}) async-start(), calls=%async_computation.3 | async-start | bytes 19464192 | tf_op jit(solution)/shard_map/all_gather | solution.py:557
  17.5 505.3 %reduce-scatter.5.cloned.1.call-start = ((), (), s32[]{:S(2)}) async-start(), calls=%async_computation.5 | async-start | bytes 6488064 | tf_op jit(solution)/shard_map/reduce_scatter | solution.py:652
  17.6 22.0 %collective-permute-start.1 = (bf16[128,2048]{1,0:T(8,128)(2,1)S(1)}, bf16[128,2048]{1,0:T(8,128)(2,1)}, u32[]{:S(2)}, u32[]{:S(2)}) collective-permute-start(bf16[128,2048]{1,0:T(8,128)(2,1)S(1)} %copy-done.27), channel_id=1, source_target_pairs={{0,32},{32,64},{64,96},{96,0},{1,33},{33,65},{65,97},{97,1},{2,34}... | collective-permute-start | bytes 1572872 | tf_op jit(solution)/shard_map/ppermute | solution.py:21
  18.8 28.7 %collective-permute-start = (bf16[128,2048]{1,0:T(8,128)(2,1)S(1)}, bf16[128,2048]{1,0:T(8,128)(2,1)}, u32[]{:S(2)}, u32[]{:S(2)}) collective-permute-start(bf16[128,2048]{1,0:T(8,128)(2,1)S(1)} %copy-done.27), channel_id=1, source_target_pairs={{0,96},{32,0},{64,32},{96,64},{1,97},{33,1},{65,33},{97,65},{2,98}... | collective-permute-start | bytes 1572872 | tf_op jit(solution)/shard_map/ppermute | solution.py:21
  19.7 17.9 %collective-permute-start.4 = (bf16[16,2048]{1,0:T(8,128)(2,1)S(1)}, bf16[16,2048]{1,0:T(8,128)(2,1)}, u32[]{:S(2)}, u32[]{:S(2)}) collective-permute-start(bf16[16,2048]{1,0:T(8,128)(2,1)S(1)} %slice.562), channel_id=1, source_target_pairs={{0,1},{1,2},{2,3},{3,4},{4,5},{5,6},{6,7},{7,8},{8,9},{9,10},{10,1... | collective-permute-start | bytes 196616 | tf_op jit(solution)/shard_map/ppermute | solution.py:597
  38.8 8.7 %collective-permute-start.5 = (bf16[16,2048]{1,0:T(8,128)(2,1)}, bf16[16,2048]{1,0:T(8,128)(2,1)S(1)}, u32[]{:S(2)}, u32[]{:S(2)}) collective-permute-start(bf16[16,2048]{1,0:T(8,128)(2,1)} %collective-permute-done.4), channel_id=1, source_target_pairs={{0,96},{32,0},{64,32},{96,64},{1,97},{33,1},{65,33},{97,65},{2,98}... | collective-permute-start | bytes 196616 | tf_op jit(solution)/shard_map/ppermute | solution.py:21
  41.3 8.8 %collective-permute-start.2 = (bf16[64,2048]{1,0:T(8,128)(2,1)}, bf16[64,2048]{1,0:T(8,128)(2,1)}, u32[]{:S(2)}, u32[]{:S(2)}) collective-permute-start(bf16[64,2048]{1,0:T(8,128)(2,1)} %slice.720), channel_id=1, source_target_pairs={{0,32},{32,64},{64,96},{96,0},{1,33},{33,65},{65,97},{97,1},{2,34}... | collective-permute-start | bytes 786440 | tf_op jit(solution)/shard_map/ppermute | solution.py:21
  44.5 12.9 %collective-permute-start.7 = (bf16[8,2048]{1,0:T(8,128)(2,1)S(1)}, bf16[8,2048]{1,0:T(8,128)(2,1)S(1)}, u32[]{:S(2)}, u32[]{:S(2)}) collective-permute-start(bf16[8,2048]{1,0:T(8,128)(2,1)S(1)} %slice.722), channel_id=1, source_target_pairs={{0,32},{32,64},{64,96},{96,0},{1,33},{33,65},{65,97},{97,1},{2,34}... | collective-permute-start | bytes 98312 | tf_op jit(solution)/shard_map/ppermute | solution.py:21
  47.5 9.9 %collective-permute-start.8 = (bf16[8,2048]{1,0:T(8,128)(2,1)S(1)}, bf16[8,2048]{1,0:T(8,128)(2,1)S(1)}, u32[]{:S(2)}, u32[]{:S(2)}) collective-permute-start(bf16[8,2048]{1,0:T(8,128)(2,1)S(1)} %slice.723), channel_id=1, source_target_pairs={{0,96},{32,0},{64,32},{96,64},{1,97},{33,1},{65,33},{97,65},{2,98}... | collective-permute-start | bytes 98312 | tf_op jit(solution)/shard_map/ppermute | solution.py:21
  123.0 12.1 %collective-permute-start.14 = (f32[4,2,8,640]{3,2,1,0:T(8,128)S(1)}, f32[4,2,8,640]{3,2,1,0:T(8,128)S(1)}, u32[]{:S(2)}, u32[]{:S(2)}) collective-permute-start(f32[4,2,8,640]{3,2,1,0:T(8,128)S(1)} %get-tuple-element.168), channel_id=1, source_target_pairs={{0,16},{1,17},{2,18},{3,19},{4,20},{5,21},{6,22},{7,23},{8,24},{9,... | collective-permute-start | bytes 491528 | tf_op jit(solution)/shard_map/ppermute | solution.py:38
  125.0 15.5 %collective-permute-start.13 = (f32[4,2,8,640]{3,2,1,0:T(8,128)S(1)}, f32[4,2,8,640]{3,2,1,0:T(8,128)S(1)}, u32[]{:S(2)}, u32[]{:S(2)}) collective-permute-start(f32[4,2,8,640]{3,2,1,0:T(8,128)S(1)} %get-tuple-element.168), channel_id=1, source_target_pairs={{0,24},{1,25},{2,26},{3,27},{4,28},{5,29},{6,30},{7,31},{8,0},{9,1... | collective-permute-start | bytes 491528 | tf_op jit(solution)/shard_map/ppermute | solution.py:38
  126.2 14.4 %collective-permute-start.15 = (f32[4,2,8,640]{3,2,1,0:T(8,128)S(1)}, f32[4,2,8,640]{3,2,1,0:T(8,128)S(1)}, u32[]{:S(2)}, u32[]{:S(2)}) collective-permute-start(f32[4,2,8,640]{3,2,1,0:T(8,128)S(1)} %get-tuple-element.168), channel_id=1, source_target_pairs={{0,8},{1,9},{2,10},{3,11},{4,12},{5,13},{6,14},{7,15},{8,16},{9,17... | collective-permute-start | bytes 491528 | tf_op jit(solution)/shard_map/ppermute | solution.py:38
  146.7 9.3 %collective-permute-start.16 = (bf16[64,2048]{1,0:T(8,128)(2,1)S(1)}, bf16[64,2048]{1,0:T(8,128)(2,1)S(1)}, u32[]{:S(2)}, u32[]{:S(2)}) collective-permute-start(bf16[64,2048]{1,0:T(8,128)(2,1)S(1)} %get-tuple-element.95), channel_id=1, source_target_pairs={{0,32},{32,64},{64,96},{96,0},{1,33},{33,65},{65,97},{97,1},{2,34}... | collective-permute-start | bytes 786440 | tf_op jit(solution)/shard_map/ppermute | solution.py:21
  147.9 9.2 %collective-permute-start.18 = (bf16[64,2048]{1,0:T(8,128)(2,1)S(1)}, bf16[64,2048]{1,0:T(8,128)(2,1)S(1)}, u32[]{:S(2)}, u32[]{:S(2)}) collective-permute-start(bf16[64,2048]{1,0:T(8,128)(2,1)S(1)} %get-tuple-element.96), channel_id=1, source_target_pairs={{0,96},{32,0},{64,32},{96,64},{1,97},{33,1},{65,33},{97,65},{2,98}... | collective-permute-start | bytes 786440 | tf_op jit(solution)/shard_map/ppermute | solution.py:21
  148.8 19.6 %collective-permute-start.28 = (bf16[128,2048]{1,0:T(8,128)(2,1)S(1)}, bf16[128,2048]{1,0:T(8,128)(2,1)S(1)}, u32[]{:S(2)}, u32[]{:S(2)}) collective-permute-start(bf16[128,2048]{1,0:T(8,128)(2,1)S(1)} %copy-done.40), channel_id=1, source_target_pairs={{0,96},{32,0},{64,32},{96,64},{1,97},{33,1},{65,33},{97,65},{2,98}... | collective-permute-start | bytes 1572872 | tf_op jit(solution)/shard_map/ppermute | solution.py:21
  149.4 20.7 %collective-permute-start.29 = (bf16[128,2048]{1,0:T(8,128)(2,1)S(1)}, bf16[128,2048]{1,0:T(8,128)(2,1)S(1)}, u32[]{:S(2)}, u32[]{:S(2)}) collective-permute-start(bf16[128,2048]{1,0:T(8,128)(2,1)S(1)} %copy-done.40), channel_id=1, source_target_pairs={{0,32},{32,64},{64,96},{96,0},{1,33},{33,65},{65,97},{97,1},{2,34}... | collective-permute-start | bytes 1572872 | tf_op jit(solution)/shard_map/ppermute | solution.py:21
  157.4 22.0 %collective-permute-start.19 = (bf16[128,2048]{1,0:T(8,128)(2,1)S(1)}, bf16[128,2048]{1,0:T(8,128)(2,1)}, u32[]{:S(2)}, u32[]{:S(2)}) collective-permute-start(bf16[128,2048]{1,0:T(8,128)(2,1)S(1)} %pad_maximum_fusion.8), channel_id=1, source_target_pairs={{0,96},{32,0},{64,32},{96,64},{1,97},{33,1},{65,33},{97,65},{2,98}... | collective-permute-start | bytes 1572872 | tf_op jit(solution)/shard_map/ppermute | solution.py:21
  158.3 21.0 %collective-permute-start.17 = (bf16[128,2048]{1,0:T(8,128)(2,1)S(1)}, bf16[128,2048]{1,0:T(8,128)(2,1)}, u32[]{:S(2)}, u32[]{:S(2)}) collective-permute-start(bf16[128,2048]{1,0:T(8,128)(2,1)S(1)} %pad_maximum_fusion.7), channel_id=1, source_target_pairs={{0,32},{32,64},{64,96},{96,0},{1,33},{33,65},{65,97},{97,1},{2,34}... | collective-permute-start | bytes 1572872 | tf_op jit(solution)/shard_map/ppermute | solution.py:21
  169.2 16.4 %collective-permute-start.31 = (bf16[64,2048]{1,0:T(8,128)(2,1)}, bf16[64,2048]{1,0:T(8,128)(2,1)}, u32[]{:S(2)}, u32[]{:S(2)}) collective-permute-start(bf16[64,2048]{1,0:T(8,128)(2,1)} %slice.759), channel_id=1, source_target_pairs={{0,96},{32,0},{64,32},{96,64},{1,97},{33,1},{65,33},{97,65},{2,98}... | collective-permute-start | bytes 786440 | tf_op jit(solution)/shard_map/ppermute | solution.py:21
  171.6 13.0 %collective-permute-start.30 = (bf16[64,2048]{1,0:T(8,128)(2,1)}, bf16[64,2048]{1,0:T(8,128)(2,1)}, u32[]{:S(2)}, u32[]{:S(2)}) collective-permute-start(bf16[64,2048]{1,0:T(8,128)(2,1)} %slice.758), channel_id=1, source_target_pairs={{0,32},{32,64},{64,96},{96,0},{1,33},{33,65},{65,97},{97,1},{2,34}... | collective-permute-start | bytes 786440 | tf_op jit(solution)/shard_map/ppermute | solution.py:21
  182.4 12.0 %collective-permute-start.21 = (bf16[128,2048]{1,0:T(8,128)(2,1)S(1)}, bf16[128,2048]{1,0:T(8,128)(2,1)S(1)}, u32[]{:S(2)}, u32[]{:S(2)}) collective-permute-start(bf16[128,2048]{1,0:T(8,128)(2,1)S(1)} %get-tuple-element.67), channel_id=1, source_target_pairs={{0,32},{32,64},{64,96},{96,0},{1,33},{33,65},{65,97},{97,1},{2,34}... | collective-permute-start | bytes 1572872 | tf_op jit(solution)/shard_map/ppermute | solution.py:21
  184.3 12.1 %collective-permute-start.20 = (bf16[128,2048]{1,0:T(8,128)(2,1)S(1)}, bf16[128,2048]{1,0:T(8,128)(2,1)S(1)}, u32[]{:S(2)}, u32[]{:S(2)}) collective-permute-start(bf16[128,2048]{1,0:T(8,128)(2,1)S(1)} %get-tuple-element.67), channel_id=1, source_target_pairs={{0,96},{32,0},{64,32},{96,64},{1,97},{33,1},{65,33},{97,65},{2,98}... | collective-permute-start | bytes 1572872 | tf_op jit(solution)/shard_map/ppermute | solution.py:21
  233.2 291.4 %reduce-scatter.3.cloned.1.call-start = ((), (), s32[]{:S(2)}) async-start(), calls=%async_computation.4 | async-start | bytes 12976128 | tf_op jit(solution)/shard_map/reduce_scatter | solution.py:649
  239.4 15.3 %collective-permute-start.24 = (bf16[64,2048]{1,0:T(8,128)(2,1)S(1)}, bf16[64,2048]{1,0:T(8,128)(2,1)S(1)}, u32[]{:S(2)}, u32[]{:S(2)}) collective-permute-start(bf16[64,2048]{1,0:T(8,128)(2,1)S(1)} %get-tuple-element.91), channel_id=1, source_target_pairs={{0,32},{32,64},{64,96},{96,0},{1,33},{33,65},{65,97},{97,1},{2,34}... | collective-permute-start | bytes 786440 | tf_op jit(solution)/shard_map/ppermute | solution.py:21
  240.9 13.7 %collective-permute-start.26 = (bf16[64,2048]{1,0:T(8,128)(2,1)S(1)}, bf16[64,2048]{1,0:T(8,128)(2,1)S(1)}, u32[]{:S(2)}, u32[]{:S(2)}) collective-permute-start(bf16[64,2048]{1,0:T(8,128)(2,1)S(1)} %get-tuple-element.92), channel_id=1, source_target_pairs={{0,96},{32,0},{64,32},{96,64},{1,97},{33,1},{65,33},{97,65},{2,98}... | collective-permute-start | bytes 786440 | tf_op jit(solution)/shard_map/ppermute | solution.py:21
  252.5 9.3 %collective-permute-start.32 = (bf16[64,2048]{1,0:T(8,128)(2,1)S(1)}, bf16[64,2048]{1,0:T(8,128)(2,1)S(1)}, u32[]{:S(2)}, u32[]{:S(2)}) collective-permute-start(bf16[64,2048]{1,0:T(8,128)(2,1)S(1)} %get-tuple-element.87), channel_id=1, source_target_pairs={{0,32},{32,64},{64,96},{96,0},{1,33},{33,65},{65,97},{97,1},{2,34}... | collective-permute-start | bytes 786440 | tf_op jit(solution)/shard_map/ppermute | solution.py:21
  254.1 9.2 %collective-permute-start.34 = (bf16[64,2048]{1,0:T(8,128)(2,1)S(1)}, bf16[64,2048]{1,0:T(8,128)(2,1)S(1)}, u32[]{:S(2)}, u32[]{:S(2)}) collective-permute-start(bf16[64,2048]{1,0:T(8,128)(2,1)S(1)} %get-tuple-element.88), channel_id=1, source_target_pairs={{0,96},{32,0},{64,32},{96,64},{1,97},{33,1},{65,33},{97,65},{2,98}... | collective-permute-start | bytes 786440 | tf_op jit(solution)/shard_map/ppermute | solution.py:21
  254.8 17.0 %collective-permute-start.27 = (bf16[128,2048]{1,0:T(8,128)(2,1)S(1)}, bf16[128,2048]{1,0:T(8,128)(2,1)S(1)}, u32[]{:S(2)}, u32[]{:S(2)}) collective-permute-start(bf16[128,2048]{1,0:T(8,128)(2,1)S(1)} %pad_maximum_fusion.10), channel_id=1, source_target_pairs={{0,96},{32,0},{64,32},{96,64},{1,97},{33,1},{65,33},{97,65},{2,98}... | collective-permute-start | bytes 1572872 | tf_op jit(solution)/shard_map/ppermute | solution.py:21
  255.4 16.4 %collective-permute-start.25 = (bf16[128,2048]{1,0:T(8,128)(2,1)S(1)}, bf16[128,2048]{1,0:T(8,128)(2,1)S(1)}, u32[]{:S(2)}, u32[]{:S(2)}) collective-permute-start(bf16[128,2048]{1,0:T(8,128)(2,1)S(1)} %pad_maximum_fusion.9), channel_id=1, source_target_pairs={{0,32},{32,64},{64,96},{96,0},{1,33},{33,65},{65,97},{97,1},{2,34}... | collective-permute-start | bytes 1572872 | tf_op jit(solution)/shard_map/ppermute | solution.py:21
  263.5 13.9 %collective-permute-start.35 = (bf16[128,2048]{1,0:T(8,128)(2,1)S(1)}, bf16[128,2048]{1,0:T(8,128)(2,1)S(1)}, u32[]{:S(2)}, u32[]{:S(2)}) collective-permute-start(bf16[128,2048]{1,0:T(8,128)(2,1)S(1)} %pad_maximum_fusion.12), channel_id=1, source_target_pairs={{0,96},{32,0},{64,32},{96,64},{1,97},{33,1},{65,33},{97,65},{2,98}... | collective-permute-start | bytes 1572872 | tf_op jit(solution)/shard_map/ppermute | solution.py:21
  264.2 13.2 %collective-permute-start.33 = (bf16[128,2048]{1,0:T(8,128)(2,1)S(1)}, bf16[128,2048]{1,0:T(8,128)(2,1)S(1)}, u32[]{:S(2)}, u32[]{:S(2)}) collective-permute-start(bf16[128,2048]{1,0:T(8,128)(2,1)S(1)} %pad_maximum_fusion.11), channel_id=1, source_target_pairs={{0,32},{32,64},{64,96},{96,0},{1,33},{33,65},{65,97},{97,1},{2,34}... | collective-permute-start | bytes 1572872 | tf_op jit(solution)/shard_map/ppermute | solution.py:21
  280.5 12.8 %collective-permute-start.37 = (bf16[128,2048]{1,0:T(8,128)(2,1)}, bf16[128,2048]{1,0:T(8,128)(2,1)S(1)}, u32[]{:S(2)}, u32[]{:S(2)}) collective-permute-start(bf16[128,2048]{1,0:T(8,128)(2,1)} %get-tuple-element.64), channel_id=1, source_target_pairs={{0,32},{32,64},{64,96},{96,0},{1,33},{33,65},{65,97},{97,1},{2,34}... | collective-permute-start | bytes 1572872 | tf_op jit(solution)/shard_map/ppermute | solution.py:21
  283.5 25.6 %collective-permute-start.36 = (bf16[128,2048]{1,0:T(8,128)(2,1)}, bf16[128,2048]{1,0:T(8,128)(2,1)S(1)}, u32[]{:S(2)}, u32[]{:S(2)}) collective-permute-start(bf16[128,2048]{1,0:T(8,128)(2,1)} %get-tuple-element.64), channel_id=1, source_target_pairs={{0,96},{32,0},{64,32},{96,64},{1,97},{33,1},{65,33},{97,65},{2,98}... | collective-permute-start | bytes 1572872 | tf_op jit(solution)/shard_map/ppermute | solution.py:21
  294.0 16.0 %collective-permute-start.38 = (bf16[64,2048]{1,0:T(8,128)(2,1)}, bf16[64,2048]{1,0:T(8,128)(2,1)}, u32[]{:S(2)}, u32[]{:S(2)}) collective-permute-start(bf16[64,2048]{1,0:T(8,128)(2,1)} %slice.767), channel_id=1, source_target_pairs={{0,32},{32,64},{64,96},{96,0},{1,33},{33,65},{65,97},{97,1},{2,34}... | collective-permute-start | bytes 786440 | tf_op jit(solution)/shard_map/ppermute | solution.py:21
  329.1 14.0 %collective-permute-start.42 = (f32[2,8,640]{2,1,0:T(8,128)S(1)}, f32[2,8,640]{2,1,0:T(8,128)S(1)}, u32[]{:S(2)}, u32[]{:S(2)}) collective-permute-start(f32[2,8,640]{2,1,0:T(8,128)S(1)} %get-tuple-element.172), channel_id=1, source_target_pairs={{0,4},{1,5},{2,6},{3,7},{4,0},{5,1},{6,2},{7,3},{8,12},{9,13},{10,... | collective-permute-start | bytes 122888 | tf_op jit(solution)/shard_map/ppermute | solution.py:38
  330.0 13.0 %collective-permute-start.41 = (f32[2,8,640]{2,1,0:T(8,128)S(1)}, f32[2,8,640]{2,1,0:T(8,128)S(1)}, u32[]{:S(2)}, u32[]{:S(2)}) collective-permute-start(f32[2,8,640]{2,1,0:T(8,128)S(1)} %get-tuple-element.172), channel_id=1, source_target_pairs={{0,6},{1,7},{2,0},{3,1},{4,2},{5,3},{6,4},{7,5},{8,14},{9,15},{10,... | collective-permute-start | bytes 122888 | tf_op jit(solution)/shard_map/ppermute | solution.py:38
  331.8 11.3 %collective-permute-start.43 = (f32[2,8,640]{2,1,0:T(8,128)S(1)}, f32[2,8,640]{2,1,0:T(8,128)S(1)}, u32[]{:S(2)}, u32[]{:S(2)}) collective-permute-start(f32[2,8,640]{2,1,0:T(8,128)S(1)} %get-tuple-element.172), channel_id=1, source_target_pairs={{0,2},{1,3},{2,4},{3,5},{4,6},{5,7},{6,0},{7,1},{8,10},{9,11},{10,... | collective-permute-start | bytes 122888 | tf_op jit(solution)/shard_map/ppermute | solution.py:38
  343.1 8.7 %collective-permute-start.45 = (f32[4,2,8,640]{3,2,1,0:T(8,128)S(1)}, f32[4,2,8,640]{3,2,1,0:T(8,128)S(1)}, u32[]{:S(2)}, u32[]{:S(2)}) collective-permute-start(f32[4,2,8,640]{3,2,1,0:T(8,128)S(1)} %get-tuple-element.166), channel_id=1, source_target_pairs={{0,16},{1,17},{2,18},{3,19},{4,20},{5,21},{6,22},{7,23},{8,24},{9,... | collective-permute-start | bytes 491528 | tf_op jit(solution)/shard_map/ppermute | solution.py:38
  345.3 7.7 %collective-permute-start.44 = (f32[4,2,8,640]{3,2,1,0:T(8,128)S(1)}, f32[4,2,8,640]{3,2,1,0:T(8,128)S(1)}, u32[]{:S(2)}, u32[]{:S(2)}) collective-permute-start(f32[4,2,8,640]{3,2,1,0:T(8,128)S(1)} %get-tuple-element.166), channel_id=1, source_target_pairs={{0,24},{1,25},{2,26},{3,27},{4,28},{5,29},{6,30},{7,31},{8,0},{9,1... | collective-permute-start | bytes 491528 | tf_op jit(solution)/shard_map/ppermute | solution.py:38
  347.3 7.0 %collective-permute-start.46 = (f32[4,2,8,640]{3,2,1,0:T(8,128)S(1)}, f32[4,2,8,640]{3,2,1,0:T(8,128)S(1)}, u32[]{:S(2)}, u32[]{:S(2)}) collective-permute-start(f32[4,2,8,640]{3,2,1,0:T(8,128)S(1)} %get-tuple-element.166), channel_id=1, source_target_pairs={{0,8},{1,9},{2,10},{3,11},{4,12},{5,13},{6,14},{7,15},{8,16},{9,17... | collective-permute-start | bytes 491528 | tf_op jit(solution)/shard_map/ppermute | solution.py:38
  351.2 129.8 %collective-permute-start.62 = (bf16[4,4,64,1280]{3,2,1,0:T(8,128)(2,1)}, bf16[4,4,64,1280]{3,2,1,0:T(8,128)(2,1)}, u32[]{:S(2)}, u32[]{:S(2)}) collective-permute-start(bf16[4,4,64,1280]{3,2,1,0:T(8,128)(2,1)} %dynamic-slice_bitcast_fusion), channel_id=1, source_target_pairs={{0,1},{1,0},{2,3},{3,2},{4,5},{5,4},{6,7},{7,6},{8,9},{9,8},{10,11... | collective-permute-start | bytes 7864328 | tf_op jit(solution)/shard_map/ppermute | solution.py:38
  387.0 7.6 %collective-permute-start.48 = (bf16[64,2048]{1,0:T(8,128)(2,1)}, bf16[64,2048]{1,0:T(8,128)(2,1)S(1)}, u32[]{:S(2)}, u32[]{:S(2)}) collective-permute-start(bf16[64,2048]{1,0:T(8,128)(2,1)} %get-tuple-element.83), channel_id=1, source_target_pairs={{0,32},{32,64},{64,96},{96,0},{1,33},{33,65},{65,97},{97,1},{2,34}... | collective-permute-start | bytes 786440 | tf_op jit(solution)/shard_map/ppermute | solution.py:21
  398.5 11.3 %collective-permute-start.51 = (bf16[128,2048]{1,0:T(8,128)(2,1)S(1)}, bf16[128,2048]{1,0:T(8,128)(2,1)S(1)}, u32[]{:S(2)}, u32[]{:S(2)}) collective-permute-start(bf16[128,2048]{1,0:T(8,128)(2,1)S(1)} %pad_maximum_fusion.14), channel_id=1, source_target_pairs={{0,96},{32,0},{64,32},{96,64},{1,97},{33,1},{65,33},{97,65},{2,98}... | collective-permute-start | bytes 1572872 | tf_op jit(solution)/shard_map/ppermute | solution.py:21
  398.9 11.1 %collective-permute-start.49 = (bf16[128,2048]{1,0:T(8,128)(2,1)S(1)}, bf16[128,2048]{1,0:T(8,128)(2,1)S(1)}, u32[]{:S(2)}, u32[]{:S(2)}) collective-permute-start(bf16[128,2048]{1,0:T(8,128)(2,1)S(1)} %pad_maximum_fusion.13), channel_id=1, source_target_pairs={{0,32},{32,64},{64,96},{96,0},{1,33},{33,65},{65,97},{97,1},{2,34}... | collective-permute-start | bytes 1572872 | tf_op jit(solution)/shard_map/ppermute | solution.py:21
  403.9 18.9 %collective-permute-start.71 = (bf16[4,4,64,640]{3,2,1,0:T(8,128)(2,1)}, bf16[4,4,64,640]{3,2,1,0:T(8,128)(2,1)}, u32[]{:S(2)}, u32[]{:S(2)}) collective-permute-start(bf16[4,4,64,640]{3,2,1,0:T(8,128)(2,1)} %dynamic-slice_bitcast_fusion.1), channel_id=1, source_target_pairs={{0,1},{1,0},{2,3},{3,2},{4,5},{5,4},{6,7},{7,6},{8,9},{9,8},{10,11... | collective-permute-start | bytes 3932168 | tf_op jit(solution)/shard_map/ppermute | solution.py:38
  417.9 9.2 %collective-permute-start.53 = (f32[4,6688]{1,0:T(4,128)S(1)}, f32[4,6688]{1,0:T(4,128)S(1)}, u32[]{:S(2)}, u32[]{:S(2)}) collective-permute-start(f32[4,6688]{1,0:T(4,128)S(1)} %get-tuple-element.136), channel_id=1, source_target_pairs={{0,8},{1,9},{2,10},{3,11},{4,12},{5,13},{6,14},{7,15},{8,16},{9,17... | collective-permute-start | bytes 321032 | tf_op jit(solution)/shard_map/ppermute | solution.py:38
  418.6 8.5 %collective-permute-start.55 = (f32[4,6688]{1,0:T(4,128)S(1)}, f32[4,6688]{1,0:T(4,128)S(1)}, u32[]{:S(2)}, u32[]{:S(2)}) collective-permute-start(f32[4,6688]{1,0:T(4,128)S(1)} %get-tuple-element.137), channel_id=1, source_target_pairs={{0,24},{1,25},{2,26},{3,27},{4,28},{5,29},{6,30},{7,31},{8,0},{9,1... | collective-permute-start | bytes 321032 | tf_op jit(solution)/shard_map/ppermute | solution.py:38
  421.2 9.8 %collective-permute-start.54 = (f32[4,6688]{1,0:T(4,128)S(1)}, f32[4,6688]{1,0:T(4,128)S(1)}, u32[]{:S(2)}, u32[]{:S(2)}) collective-permute-start(f32[4,6688]{1,0:T(4,128)S(1)} %get-tuple-element.138), channel_id=1, source_target_pairs={{0,16},{1,17},{2,18},{3,19},{4,20},{5,21},{6,22},{7,23},{8,24},{9,... | collective-permute-start | bytes 321032 | tf_op jit(solution)/shard_map/ppermute | solution.py:38
  425.0 28.6 %collective-permute-start.72 = (bf16[128,320]{1,0:T(8,128)(2,1)S(1)}, bf16[128,320]{1,0:T(8,128)(2,1)S(1)}, u32[]{:S(2)}, u32[]{:S(2)}) collective-permute-start(bf16[128,320]{1,0:T(8,128)(2,1)S(1)} %get-tuple-element.118), channel_id=1, source_target_pairs={{0,2},{1,3},{2,4},{3,5},{4,6},{5,7},{6,0},{7,1},{8,10},{9,11},{10,... | collective-permute-start | bytes 245768 | tf_op jit(solution)/shard_map/ppermute | solution.py:38
  440.2 7.4 %collective-permute-start.60 = (f32[128]{0:T(128)S(1)}, f32[128]{0:T(128)S(1)}, u32[]{:S(2)}, u32[]{:S(2)}) collective-permute-start(f32[128]{0:T(128)S(1)} %concatenate.175), channel_id=1, source_target_pairs={{0,96},{32,0},{64,32},{96,64},{1,97},{33,1},{65,33},{97,65},{2,98}... | collective-permute-start | bytes 1544 | tf_op jit(solution)/shard_map/ppermute | solution.py:21
  441.0 8.7 %collective-permute-start.61 = (f32[128]{0:T(128)S(1)}, f32[128]{0:T(128)S(1)}, u32[]{:S(2)}, u32[]{:S(2)}) collective-permute-start(f32[128]{0:T(128)S(1)} %concatenate.175), channel_id=1, source_target_pairs={{0,64},{32,96},{64,0},{96,32},{1,65},{33,97},{65,1},{97,33},{2,66}... | collective-permute-start | bytes 1544 | tf_op jit(solution)/shard_map/ppermute | solution.py:21
  449.7 7.1 %collective-permute-start.80 = (bf16[128,320]{1,0:T(8,128)(2,1)S(1)}, bf16[128,320]{1,0:T(8,128)(2,1)S(1)}, u32[]{:S(2)}, u32[]{:S(2)}) collective-permute-start(bf16[128,320]{1,0:T(8,128)(2,1)S(1)} %get-tuple-element.124), channel_id=1, source_target_pairs={{0,8},{1,9},{2,10},{3,11},{4,12},{5,13},{6,14},{7,15},{8,16},{9,17... | collective-permute-start | bytes 245768 | tf_op jit(solution)/shard_map/ppermute | solution.py:38
  456.9 10.2 %collective-permute-start.83 = (bf16[256,320]{1,0:T(8,128)(2,1)S(1)}, bf16[256,320]{1,0:T(8,128)(2,1)S(1)}, u32[]{:S(2)}, u32[]{:S(2)}) collective-permute-start(bf16[256,320]{1,0:T(8,128)(2,1)S(1)} %pad_maximum_fusion.23), channel_id=1, source_target_pairs={{0,24},{1,25},{2,26},{3,27},{4,28},{5,29},{6,30},{7,31},{8,0},{9,1... | collective-permute-start | bytes 491528 | tf_op jit(solution)/shard_map/ppermute | solution.py:38
  484.8 7.6 %collective-permute-start.88 = (bf16[128,640]{1,0:T(8,128)(2,1)S(1)}, bf16[128,640]{1,0:T(8,128)(2,1)S(1)}, u32[]{:S(2)}, u32[]{:S(2)}) collective-permute-start(bf16[128,640]{1,0:T(8,128)(2,1)S(1)} %get-tuple-element.101), channel_id=1, source_target_pairs={{0,8},{1,9},{2,10},{3,11},{4,12},{5,13},{6,14},{7,15},{8,16},{9,17... | collective-permute-start | bytes 491528 | tf_op jit(solution)/shard_map/ppermute | solution.py:38
  484.9 7.6 %collective-permute-start.90 = (bf16[128,640]{1,0:T(8,128)(2,1)S(1)}, bf16[128,640]{1,0:T(8,128)(2,1)S(1)}, u32[]{:S(2)}, u32[]{:S(2)}) collective-permute-start(bf16[128,640]{1,0:T(8,128)(2,1)S(1)} %get-tuple-element.103), channel_id=1, source_target_pairs={{0,24},{1,25},{2,26},{3,27},{4,28},{5,29},{6,30},{7,31},{8,0},{9,1... | collective-permute-start | bytes 491528 | tf_op jit(solution)/shard_map/ppermute | solution.py:38
  489.1 7.3 %collective-permute-start.63 = (bf16[128,640]{1,0:T(8,128)(2,1)S(1)}, bf16[128,640]{1,0:T(8,128)(2,1)S(1)}, u32[]{:S(2)}, u32[]{:S(2)}) collective-permute-start(bf16[128,640]{1,0:T(8,128)(2,1)S(1)} %get-tuple-element.109), channel_id=1, source_target_pairs={{0,2},{1,3},{2,4},{3,5},{4,6},{5,7},{6,0},{7,1},{8,10},{9,11},{10,... | collective-permute-start | bytes 491528 | tf_op jit(solution)/shard_map/ppermute | solution.py:38
  489.2 7.3 %collective-permute-start.65 = (bf16[128,640]{1,0:T(8,128)(2,1)S(1)}, bf16[128,640]{1,0:T(8,128)(2,1)S(1)}, u32[]{:S(2)}, u32[]{:S(2)}) collective-permute-start(bf16[128,640]{1,0:T(8,128)(2,1)S(1)} %get-tuple-element.111), channel_id=1, source_target_pairs={{0,6},{1,7},{2,0},{3,1},{4,2},{5,3},{6,4},{7,5},{8,14},{9,15},{10,... | collective-permute-start | bytes 491528 | tf_op jit(solution)/shard_map/ppermute | solution.py:38
  492.6 7.6 %collective-permute-start.91 = (bf16[256,640]{1,0:T(8,128)(2,1)S(1)}, bf16[256,640]{1,0:T(8,128)(2,1)S(1)}, u32[]{:S(2)}, u32[]{:S(2)}) collective-permute-start(bf16[256,640]{1,0:T(8,128)(2,1)S(1)} %pad_maximum_fusion.18), channel_id=1, source_target_pairs={{0,24},{1,25},{2,26},{3,27},{4,28},{5,29},{6,30},{7,31},{8,0},{9,1... | collective-permute-start | bytes 983048 | tf_op jit(solution)/shard_map/ppermute | solution.py:38
  494.9 8.4 %collective-permute-start.89 = (bf16[256,640]{1,0:T(8,128)(2,1)S(1)}, bf16[256,640]{1,0:T(8,128)(2,1)S(1)}, u32[]{:S(2)}, u32[]{:S(2)}) collective-permute-start(bf16[256,640]{1,0:T(8,128)(2,1)S(1)} %pad_maximum_fusion.17), channel_id=1, source_target_pairs={{0,8},{1,9},{2,10},{3,11},{4,12},{5,13},{6,14},{7,15},{8,16},{9,17... | collective-permute-start | bytes 983048 | tf_op jit(solution)/shard_map/ppermute | solution.py:38
  496.6 10.1 %collective-permute-start.66 = (bf16[256,640]{1,0:T(8,128)(2,1)S(1)}, bf16[256,640]{1,0:T(8,128)(2,1)S(1)}, u32[]{:S(2)}, u32[]{:S(2)}) collective-permute-start(bf16[256,640]{1,0:T(8,128)(2,1)S(1)} %pad_maximum_fusion.16), channel_id=1, source_target_pairs={{0,6},{1,7},{2,0},{3,1},{4,2},{5,3},{6,4},{7,5},{8,14},{9,15},{10,... | collective-permute-start | bytes 983048 | tf_op jit(solution)/shard_map/ppermute | solution.py:38
  499.2 8.4 %collective-permute-start.64 = (bf16[256,640]{1,0:T(8,128)(2,1)S(1)}, bf16[256,640]{1,0:T(8,128)(2,1)S(1)}, u32[]{:S(2)}, u32[]{:S(2)}) collective-permute-start(bf16[256,640]{1,0:T(8,128)(2,1)S(1)} %pad_maximum_fusion.15), channel_id=1, source_target_pairs={{0,2},{1,3},{2,4},{3,5},{4,6},{5,7},{6,0},{7,1},{8,10},{9,11},{10,... | collective-permute-start | bytes 983048 | tf_op jit(solution)/shard_map/ppermute | solution.py:38
  503.4 7.7 %collective-permute-start.92 = (bf16[32,640]{1,0:T(8,128)(2,1)S(1)}, bf16[32,640]{1,0:T(8,128)(2,1)S(1)}, u32[]{:S(2)}, u32[]{:S(2)}) collective-permute-start(bf16[32,640]{1,0:T(8,128)(2,1)S(1)} %get-tuple-element.143), channel_id=1, source_target_pairs={{0,2},{1,3},{2,4},{3,5},{4,6},{5,7},{6,0},{7,1},{8,10},{9,11},{10,... | collective-permute-start | bytes 122888 | tf_op jit(solution)/shard_map/ppermute | solution.py:38
  503.5 7.6 %collective-permute-start.94 = (bf16[32,640]{1,0:T(8,128)(2,1)S(1)}, bf16[32,640]{1,0:T(8,128)(2,1)S(1)}, u32[]{:S(2)}, u32[]{:S(2)}) collective-permute-start(bf16[32,640]{1,0:T(8,128)(2,1)S(1)} %get-tuple-element.145), channel_id=1, source_target_pairs={{0,6},{1,7},{2,0},{3,1},{4,2},{5,3},{6,4},{7,5},{8,14},{9,15},{10,... | collective-permute-start | bytes 122888 | tf_op jit(solution)/shard_map/ppermute | solution.py:38
  (94 other events, 597.1 us)
Sparse Core Ops, SparseCore 0:
  15.6 55.3 all-gather.2
  73.3 83.4 all-gather.4
  233.3 84.2 reduce-scatter.4
  321.8 109.3 reduce-scatter.2
